TPU v7x, 256 devices: a whole 4x4x8 slice. The times are simulated.
256 devices in a mesh: prompt: 2 (over x_lo), group: 16 (over z, x_hi), tensor: 8 (over y, core).
Axes of the slice: x: 4 (x_hi: 2, x_lo: 2; x = x_hi * 2 + x_lo), y: 4, z: 8, core: 2. Of those that a mesh axis runs over, the one named last changes fastest.
Arguments:
- queries: bfloat16 [32, 512, 4096], P(('prompt', 'group'), None, 'tensor'), parts along dimension 0
- response_kv: bfloat16 [32, 2, 512, 1024], P(('prompt', 'group'), None, None, 'tensor'), parts along dimension 0
- grad_out: bfloat16 [32, 512, 4096], P(('prompt', 'group'), None, 'tensor'), parts along dimension 0, may hold values from -6 to 6
- prefix_kv: bfloat16 [32, 2, 2048, 1024], P(('prompt', 'group'), None, None, 'tensor'), parts along dimension 0, may hold values from -6 to 6
- kv_weight: bfloat16 [2, 5120, 1024], P(None, None, 'tensor'), may hold values from -0.078125 to 0.078125
- resp_len: int32 [32], P(('prompt', 'group')), parts along dimension 0, may hold values from 1 to 512, 4352 in all
- prefix_len: int32 [2], P('prompt'), parts along dimension 0, may hold values from 1024 to 2048
- owner: int32 [2], P('prompt'), parts along dimension 0, may hold values from 0 to 15
Outputs:
- query_grad: bfloat16 [32, 512, 4096], P(('prompt', 'group'), None, 'tensor'), parts along dimension 0
- kv_grad: bfloat16 [32, 2, 512, 1024], P(('prompt', 'group'), None, None, 'tensor'), parts along dimension 0
- input_grad: bfloat16 [4096, 5120], P(('prompt', 'group'), 'tensor'), parts along dimension 0
There are 2 independent parts, one for each index of `prompt`. A program takes and returns all parts, laid end to end along the dimension named above; an argument that names none is the same for every part. Nothing has to cross between parts.
Inputs may be any that keep to these rules, and one draw needn't show every extreme that they name: `resp_len`: each response has 1 to 512 live positions, and some response has exactly 512. `prefix_len`: at least half of the prefix is live. Only the owner's slot of prefix_kv is read.
All inputs are finite; a program needn't handle non-finite values. No bound on the sum of `resp_len` on one device may be relied on, other than what follows from the above.
Results may differ from a plain program's by a relative error of at most 0.015.
Values may be sent and summed in bfloat16 or wider, within the bound.
No kernel may reach another device: no remote copies, remote signals or barrier semaphores. Data moves between devices by JAX's collectives and lax.ppermute only.
A program may use at most 128 MiB of HBM per device.

v0:
```python
import jax
import jax.numpy as jnp
from jax import lax
from jax.sharding import PartitionSpec as P


def broadcast(block, axis, holder):
    block = jnp.where(lax.axis_index(axis) == holder, block, jnp.zeros_like(block))
    return lax.psum(block, axis)


def project_rows(key_rows, value_rows, kv_weight):
    highest = lax.Precision.HIGHEST
    numbers = (((1,), (1,)), ((), ()))
    key_proj = kv_weight[0].astype(jnp.float32)
    value_proj = kv_weight[1].astype(jnp.float32)
    return lax.dot_general(key_rows, key_proj, numbers, precision=highest) + lax.dot_general(
        value_rows, value_proj, numbers, precision=highest
    )


def on_device(queries, response_kv, grad_out, prefix_kv, kv_weight, resp_len, prefix_len, owner):
    prefix = broadcast(prefix_kv[0], "group", owner[0])
    prefix_rows = prefix.shape[1]
    resp_rows = queries.shape[1]
    head_dim = prefix.shape[2]
    head_count = queries.shape[2] // head_dim
    scaling = head_dim ** (-0.5)
    all_keys = jnp.concatenate([prefix[0], response_kv[0, 0]], 0)
    all_values = jnp.concatenate([prefix[1], response_kv[0, 1]], 0)
    query_heads = queries[0].reshape(resp_rows, head_count, head_dim)
    grad_heads = grad_out[0].reshape(resp_rows, head_count, head_dim)
    span_rows = min(512, resp_rows)
    resp_length = resp_len[0]
    num_blocks = (resp_length + span_rows - 1) // span_rows
    key_pos = jnp.arange(prefix_rows + resp_rows)
    prefix_ok = key_pos < prefix_len[0]
    contract_last = (((1,), (1,)), ((), ()))
    contract_first = (((0,), (0,)), ((), ()))

    def per_block(index, running):
        query_acc, key_acc, value_acc = running
        row_start = index * span_rows
        row_ids = row_start + jnp.arange(span_rows)
        row_live = row_ids < resp_length
        allowed = jnp.where(
            key_pos[None, :] < prefix_rows,
            prefix_ok[None, :],
            key_pos[None, :] - prefix_rows <= row_ids[:, None],
        )
        pieces = []
        for head_index in range(head_count):
            head_query = query_heads[:, head_index]
            head_grad = grad_heads[:, head_index]
            scores = (
                lax.dot_general(
                    head_query, all_keys, contract_last, preferred_element_type=jnp.float32
                )
                * scaling
            )
            scores = jnp.where(allowed, scores, -jnp.inf)
            raised = jnp.exp(scores - jnp.max(scores, -1, keepdims=True))
            probs = raised / jnp.sum(raised, -1, keepdims=True)
            probs = jnp.where(row_live[:, None], probs, jnp.float32(0.0))
            probs_low = probs.astype(jnp.bfloat16)
            attended = jnp.dot(probs_low, all_values, preferred_element_type=jnp.float32)
            row_dot = jnp.sum(head_grad.astype(jnp.float32) * attended, -1)
            grad_probs = lax.dot_general(
                head_grad, all_values, contract_last, preferred_element_type=jnp.float32
            )
            scores_low = (probs * (grad_probs - row_dot[:, None])).astype(jnp.bfloat16)
            pieces.append(
                jnp.dot(scores_low, all_keys, preferred_element_type=jnp.float32) * scaling
            )
            key_acc = (
                key_acc
                + lax.dot_general(
                    scores_low, head_query, contract_first, preferred_element_type=jnp.float32
                )
                * scaling
            )
            value_acc = value_acc + lax.dot_general(
                probs_low, head_grad, contract_first, preferred_element_type=jnp.float32
            )
        block_out = jnp.concatenate(pieces, 1).astype(jnp.bfloat16)
        query_acc = lax.dynamic_update_slice_in_dim(query_acc, block_out, row_start, 0)
        return (query_acc, key_acc, value_acc)

    start_query = jnp.zeros((resp_rows, head_count * head_dim), jnp.bfloat16)
    start_keys = jnp.zeros((prefix_rows + resp_rows, head_dim), jnp.float32)
    query_acc, key_acc, value_acc = lax.fori_loop(
        0, num_blocks, per_block, (start_query, start_keys, start_keys)
    )
    own_kv = jnp.stack([key_acc[prefix_rows:], value_acc[prefix_rows:]]).astype(jnp.bfloat16)
    prefix_keys = key_acc[:prefix_rows]
    prefix_values = value_acc[:prefix_rows]
    summed = lax.psum_scatter(
        jnp.stack([prefix_keys, prefix_values]), "group", scatter_dimension=1, tiled=True
    )
    shares = project_rows(summed[0], summed[1], kv_weight)
    input_grad = lax.psum_scatter(shares, "tensor", scatter_dimension=1, tiled=True).astype(
        jnp.bfloat16
    )
    return (query_acc[None], own_kv[None], input_grad)


def solution(mesh):
    in_specs = (
        P(("prompt", "group"), None, "tensor"),
        P(("prompt", "group"), None, None, "tensor"),
        P(("prompt", "group"), None, "tensor"),
        P(("prompt", "group"), None, None, "tensor"),
        P(None, None, "tensor"),
        P(("prompt", "group")),
        P("prompt"),
        P("prompt"),
    )
    out_specs = (
        P(("prompt", "group"), None, "tensor"),
        P(("prompt", "group"), None, None, "tensor"),
        P(("prompt", "group"), "tensor"),
    )
    return jax.shard_map(
        on_device, mesh=mesh, in_specs=in_specs, out_specs=out_specs, check_vma=False
    )
```

profile of v0, /device:TPU:1, one launch (start us, length us, event | category | flops | bytes accessed | tf_op | source)
XLA Modules:
  0.0 484.8 jit_solution(10730210526800450378)
XLA Ops:
  7.9 1.1 select_bitcast_fusion
  10.6 153.9 %all-reduce.2.cloned.1.call-done = bf16[2,2048,128]{2,1,0:T(8,128)(2,1)} async-done(((bf16[2,2048,128]{2,1,0:T(8,128)(2,1)}), bf16[2,2048,128]{2,1,0:T(8,128)(2,1)}) %all-reduce.2.cloned.1.call-update) | async-done | bytes 1048592 | tf_op jit(solution)/shard_map/psum | solution.py:9
  164.5 1.3 slice_bitcast_fusion.2
  165.9 0.8 broadcast_in_dim.97
  166.7 1.2 broadcast_in_dim.98.clone
  167.9 1.2 broadcast_in_dim.98
  169.1 53.6 %while.18 = (s32[]{:T(128)}, bf16[512,512]{0,1:T(8,128)(2,1)}, f32[2560,128]{1,0:T(8,128)}, f32[2560,128]{1,0:T(8,128)}, s32[]{:T(128)}, /*index=5*/s32[]{:T(128...) while((s32[]{:T(128)}, bf16[512,512]{0,1:T(8,128)(2,1)}, ...), condition=%wide.region_14.15_spmd.clone.clone, body=%wide.region_1.14_spmd.clone.clone.sunk | while | flops 8139049984 | bytes 334653824 | solution.py:91
  170.4 1.5 fusion.230
  171.9 0.8 fusion.231
  172.7 1.5 fusion.228
  174.3 0.8 fusion.229
  175.1 1.5 fusion.226
  176.6 0.8 fusion.227
  177.5 3.7 fusion.224
  181.2 3.3 fusion.225
  184.5 12.4 %divide_select_fusion.5 = (f32[512,2560]{1,0:T(8,128)}, f32[512,2560]{1,0:T(8,128)}, f32[512,2560]{1,0:T(8,128)S(1)}, f32[512,2560]{1,0:T(8,128)S(1)}) fusion(f32[512,2560]{1,0:T(8,128)} %get-tuple-element.348, f32[512]{0:T(512)S(1)} %fusion.225, f32[512]{0:T(512)S(1)} %get-tuple-element.349, pred[512]{0:T(512)(128)(4,1)S(1)} %broadcast_compare_fusion.2, ...), kind=kLoop, calls=%fused_computation.15.clone.1 | loop fusion | flops 15728640 | bytes 41959936 | tf_op jit(solution)/shard_map/while/body/jit(_where)/select_n | solution.py:64
  196.9 1.0 fusion.232
  197.9 1.0 fusion.234
  198.9 1.5 copy-done
  200.4 1.0 fusion.236
  201.4 1.5 copy-done.1
  202.9 1.0 fusion.238
  204.2 0.9 convolution_add_fusion.9
  205.1 1.2 multiply_convert_fusion.11
  206.2 0.9 convolution_add_fusion.10
  207.1 1.2 multiply_convert_fusion.10
  208.3 0.9 convolution_add_fusion.11
  209.2 1.0 multiply_convert_fusion.9
  210.2 2.0 convolution_add_fusion.12
  212.2 1.0 multiply_convert_fusion.8
  213.2 1.0 fusion.233
  214.2 0.9 convolution_multiply_fusion.11
  215.1 1.0 fusion.235
  216.1 0.9 convolution_multiply_fusion.12
  217.0 1.0 fusion.237
  218.0 0.9 convolution_multiply_fusion.13
  219.3 1.4 fusion.240
  220.8 1.0 fusion.239
  222.6 1.4 slice_bitcast_fusion
  224.3 1.5 pad_maximum_fusion.1
  225.9 207.8 %reduce-scatter.3.cloned.1.call-done = f32[2,128,128]{2,1,0:T(8,128)} async-done(((f32[2,2048,128]{2,1,0:T(8,128)}), f32[2,128,128]{2,1,0:T(8,128)}) %reduce-scatter.3.cloned.1.call-update) | async-done | bytes 131088 | tf_op jit(solution)/shard_map/reduce_scatter | solution.py:97
  433.7 2.7 fusion.85
  436.4 2.8 convolution_add_fusion.4
  439.2 1.0 copy-done.10
  440.3 1.0 copy.18
  441.3 1.0 fusion.90
  443.0 33.7 %reduce-scatter.5.cloned.1.call-done = f32[128,640]{1,0:T(8,128)} async-done(((f32[128,5120]{1,0:T(8,128)}), f32[128,640]{1,0:T(8,128)}) %reduce-scatter.5.cloned.1.call-update) | async-done | bytes 327696 | tf_op jit(solution)/shard_map/reduce_scatter | solution.py:101
  476.7 1.7 convert_element_type.89
  (46 shorter events, 4.9 us)
Async XLA Ops:
  7.2 2.7 copy-start.11
  7.2 157.4 %all-reduce.2.cloned.1.call-start = ((), (), s32[]{:S(2)}) async-start(), calls=%async_computation.2 | async-start | bytes 2097152 | tf_op jit(solution)/shard_map/psum | solution.py:9
  7.9 2.4 copy-start.12
  9.0 1.5 copy-start.13
  9.1 424.6 %reduce-scatter.3.cloned.1.call-start = ((), (), s32[]{:S(2)}) async-start(), calls=%async_computation.3 | async-start | bytes 2228224 | tf_op jit(solution)/shard_map/reduce_scatter | solution.py:97
  171.9 3.2 copy-start.2
  174.2 3.2 copy-start.3
  176.6 4.6 copy-start.4
  197.9 2.5 copy-start
  200.4 2.5 copy-start.1
  202.9 1.3 copy-start.8
  218.0 1.3 copy-start.5
  220.8 1.9 copy-start.6
  222.6 1.6 copy-start.7
  225.8 250.8 %reduce-scatter.5.cloned.1.call-start = ((), (), s32[]{:S(2)}) async-start(), calls=%async_computation.4 | async-start | bytes 2949120 | tf_op jit(solution)/shard_map/reduce_scatter | solution.py:101
  433.7 2.7 copy-start.9
  433.7 2.7 copy-start.14
  439.2 1.0 copy-start.10
Sparse Core Ops, SparseCore 0:
  10.6 153.8 all-reduce.1
  226.0 207.6 reduce-scatter.2
  439.4 37.2 reduce-scatter.4
where the time goes:
time: 487 us; the launch traced here: 485 us
  waiting for transfers between devices  395 us (81%)
  matrix products  34.9 us (7%)
  other arithmetic  25.4 us (5%)
  between operations  15.3 us (3%)
  local copies, waits for them, and re-layouts  13.5 us (3%)
    reduce_scatter x1, waiting for transfers between devices, on_device(): lax.psum_scatter(jnp.stack([prefix_keys, prefix_values]), 'group', scatte...  208 us
    psum x1, waiting for transfers between devices, broadcast(): return lax.psum(block, axis)  154 us
    reduce_scatter x1, waiting for transfers between devices, on_device(): lax.psum_scatter(shares, 'tensor', scatter_dimension=1, tiled=True)  33.7 us
    select_n x1, other arithmetic, per_block(): probs = jnp.where(row_live[:, None], probs, jnp.float32(0.0))  12.4 us
  transfers between devices with their start and end apart: 3, of which 3 were waited for; matrix products, arithmetic and copies ran while one was open for 1% of the time, Pallas kernels for 0%

commit v1 on v0

v1 whole, which is shorter than its diff:
```python
import functools

import jax
import jax.numpy as jnp
from jax import lax
from jax.experimental import pallas as pl
from jax.experimental.pallas import tpu as pltpu
from jax.sharding import PartitionSpec as P

LAST = (((1,), (1,)), ((), ()))
PLAIN = (((1,), (0,)), ((), ()))
LOG2E = 1.4426950408889634
SPLIT = 8

def dot(a, b, dims=PLAIN):
    return lax.dot_general(a, b, dims, preferred_element_type=jnp.float32)


def block_scores(kind, keys, q, scal_ref, scale2):
    s = dot(keys, q, LAST) * scale2
    at = lax.broadcasted_iota(jnp.int32, s.shape, 0)
    if kind is None:
        ok = at <= lax.broadcasted_iota(jnp.int32, s.shape, 1)
    else:
        base = lax.rem(scal_ref[2] + kind, SPLIT) * s.shape[0]
        ok = at < scal_ref[0] - base
    return jnp.where(ok, s, -jnp.inf)


def forward_kernel(kinds, scale2, first, last, scal_ref, q_ref, g_ref, *refs):
    n = len(kinds)
    kv = refs[:n]
    if first:
        out_ref = refs[n]
    else:
        in_ref, out_ref = refs[n:n + 2]
    q = q_ref[...]
    g = g_ref[...]
    if first:
        m = l = r = None
    else:
        m, l, r = in_ref[0, 0:1], in_ref[0, 1:2], in_ref[0, 2:3]
    for kind, ref in zip(kinds, kv):
        s = block_scores(kind, ref[0], q, scal_ref, scale2)
        top = jnp.max(s, 0, keepdims=True)
        new = top if m is None else jnp.maximum(m, top)
        p = jnp.exp2(s - new)
        dp = dot(ref[1], g, LAST)
        lb = jnp.sum(p, 0, keepdims=True)
        rb = jnp.sum(p * dp, 0, keepdims=True)
        if m is None:
            l, r = lb, rb
        else:
            a = jnp.exp2(m - new)
            l, r = l * a + lb, r * a + rb
        m = new
    if last:
        live = lax.broadcasted_iota(jnp.int32, m.shape, 1) < scal_ref[1]
        m = jnp.where(live, m + jnp.log2(l), jnp.inf)
        r = r / l
    out_ref[0, 0:1] = m
    out_ref[0, 1:2] = l
    out_ref[0, 2:3] = r


def forward(scal, q, g, kinds, blocks, stats, scale2, last):
    rows, width = q.shape
    dh = blocks[0].shape[2]
    heads = width // dh
    first = stats is None
    col = pl.BlockSpec((rows, dh), lambda h: (0, h))
    stat = pl.BlockSpec((1, 8, rows), lambda h: (h, 0, 0))
    full = [pl.BlockSpec(b.shape, lambda h: (0, 0, 0)) for b in blocks]
    keys = sum(b.shape[1] for b in blocks)
    return pl.pallas_call(
        functools.partial(forward_kernel, kinds, scale2, first, last),
        grid=(heads,),
        in_specs=[pl.BlockSpec(memory_space=pltpu.SMEM), col, col] + full + ([] if first else [stat]),
        out_specs=stat,
        out_shape=jax.ShapeDtypeStruct((heads, 8, rows), jnp.float32),
        cost_estimate=pl.CostEstimate(flops=4 * heads * rows * keys * dh, bytes_accessed=4 * q.size, transcendentals=heads * rows * keys),
        compiler_params=pltpu.CompilerParams(vmem_limit_bytes=48 * 2**20),
    )(scal, q, g, *blocks, *([] if first else [stats]))


def backward_kernel(kinds, scale, scale2, first, last, heads, scal_ref, q_ref, g_ref, stat_ref, *refs):
    n = len(kinds)
    kv, refs = refs[:n], refs[n:]
    if not first:
        dq_in, refs = refs[0], refs[1:]
    dq_ref, outs, accs = refs[0], refs[1:1 + n], refs[1 + n:]
    h = pl.program_id(0)
    q = q_ref[...]
    g = g_ref[...]
    mm = stat_ref[0, 0:1]
    rr = stat_ref[0, 2:3]
    dqt = None if first else dq_in[...]
    for kind, ref, out, acc in zip(kinds, kv, outs, accs):
        keys = ref[0]
        s = block_scores(kind, keys, q, scal_ref, scale2)
        p = jnp.exp2(s - mm)
        dp = dot(ref[1], g, LAST)
        ds = (p * (dp - rr)).astype(jnp.bfloat16)
        pb = p.astype(jnp.bfloat16)
        dv = dot(pb, g)
        dk = dot(ds, q)

        @pl.when(h == 0)
        def _():
            acc[0] = dk
            acc[1] = dv

        @pl.when(h != 0)
        def _():
            acc[0] += dk
            acc[1] += dv
        part = dot(keys.T, ds)
        dqt = part if dqt is None else dqt + part
    if last:
        dq_ref[...] = (dqt.T * scale).astype(dq_ref.dtype)
    else:
        dq_ref[...] = dqt

    @pl.when(h == heads - 1)
    def _():
        for out, acc in zip(outs, accs):
            out[0] = (acc[0] * scale).astype(out.dtype)
            out[1] = acc[1].astype(out.dtype)


def backward(scal, q, g, stats, kinds, blocks, dq, scale, scale2, last):
    rows, width = q.shape
    dh = blocks[0].shape[2]
    heads = width // dh
    first = dq is None
    col = pl.BlockSpec((rows, dh), lambda h: (0, h))
    stat = pl.BlockSpec((1, 8, rows), lambda h: (h, 0, 0))
    full = [pl.BlockSpec(b.shape, lambda h: (0, 0, 0)) for b in blocks]
    tall = pl.BlockSpec((dh, rows), lambda h: (h, 0))
    keys = sum(b.shape[1] for b in blocks)
    if last:
        dq_shape, dq_spec = jax.ShapeDtypeStruct((rows, width), jnp.bfloat16), col
    else:
        dq_shape, dq_spec = jax.ShapeDtypeStruct((width, rows), jnp.float32), tall
    res = pl.pallas_call(
        functools.partial(backward_kernel, kinds, scale, scale2, first, last, heads),
        grid=(heads,),
        in_specs=[pl.BlockSpec(memory_space=pltpu.SMEM), col, col, stat] + full + ([] if first else [tall]),
        out_specs=[dq_spec] + full,
        out_shape=[dq_shape] + [jax.ShapeDtypeStruct(b.shape, jnp.bfloat16) for b in blocks],
        scratch_shapes=[pltpu.VMEM(b.shape, jnp.float32) for b in blocks],
        cost_estimate=pl.CostEstimate(flops=10 * heads * rows * keys * dh, bytes_accessed=4 * q.size, transcendentals=heads * rows * keys),
        compiler_params=pltpu.CompilerParams(vmem_limit_bytes=48 * 2**20),
    )(scal, q, g, stats, *blocks, *([] if first else [dq]))
    return res[0], list(res[1:])


def ring(size, step, stride):
    block = size // stride * stride
    return [(i, (i // stride + step) * stride % block + i % stride) for i in range(size)]


def swap(size):
    return [(i, i ^ 1) for i in range(size)]


def z_hop(x, step):
    return lax.ppermute(x, "group", ring(2 * SPLIT, step, 2))


def x_swap(x):
    return lax.ppermute(x, "group", swap(2 * SPLIT))


def scatter_prefix(prefix, z, owner_z):
    keys = prefix.shape[1] // SPLIT
    is_owner = z == owner_z

    def piece(step):
        return lax.dynamic_slice_in_dim(prefix, lax.rem(z + step + SPLIT, SPLIT) * keys, keys, 1)

    up = down = None
    for left in range(SPLIT // 2, 0, -1):
        own = piece(left)
        up = z_hop(own if up is None else jnp.where(is_owner, own, up), 1)
        if left < SPLIT // 2:
            own = piece(-left)
            down = z_hop(own if down is None else jnp.where(is_owner, own, down), -1)
    away = lax.rem(z - owner_z + SPLIT, SPLIT)
    return jnp.where(is_owner, piece(0), jnp.where(away <= SPLIT // 2, up, down))


def add_low(a, b):
    return (a.astype(jnp.float32) + b.astype(jnp.float32)).astype(jnp.bfloat16)


def on_device(queries, response_kv, grad_out, prefix_kv, kv_weight, resp_len, prefix_len, owner):
    group = lax.axis_index("group")
    tensor = lax.axis_index("tensor")
    z, x, core, y = group // 2, group % 2, tensor % 2, tensor // 2
    dh = prefix_kv.shape[3]
    scale = dh ** (-0.5)
    scale2 = scale * LOG2E
    q, g, own = queries[0], grad_out[0], response_kv[0]
    scal = jnp.stack([prefix_len[0], resp_len[0], z, z]).astype(jnp.int32)

    cols = kv_weight.shape[1] // 8
    by_core = kv_weight.reshape(2, 4, 2, cols, dh)
    mine = lax.dynamic_index_in_dim(by_core, core, 2, keepdims=False)
    other = lax.ppermute(lax.dynamic_index_in_dim(by_core, 1 - core, 2, keepdims=False), "tensor", swap(8))

    stats = forward(scal, q, g, (None,), [own], None, scale2, False)

    piece = scatter_prefix(prefix_kv[0], z, owner[0] // 2)
    piece = jnp.where(x == owner[0] % 2, piece, x_swap(piece))

    pieces = {0: piece}
    stats = forward(scal, q, g, (0,), [piece], stats, scale2, False)
    up = down = piece
    for hop in range(1, SPLIT // 2 + 1):
        up = z_hop(up, 1)
        pieces[SPLIT - hop] = up
        new = [SPLIT - hop]
        if hop < SPLIT // 2:
            down = z_hop(down, -1)
            pieces[hop] = down
            new.append(hop)
        stats = forward(scal, q, g, tuple(new), [pieces[k] for k in new], stats, scale2, hop == SPLIT // 2)

    dq = up = down = None
    for left in range(SPLIT // 2, 0, -1):
        new = [left] if left == SPLIT // 2 else [left, SPLIT - left]
        dq, grads = backward(scal, q, g, stats, tuple(new), [pieces[k] for k in new], dq, scale, scale2, False)
        up = z_hop(grads[0] if up is None else add_low(grads[0], up), 1)
        if len(new) > 1:
            down = z_hop(grads[1] if down is None else add_low(grads[1], down), -1)
    dq, (last,) = backward(scal, q, g, stats, (0,), [pieces[0]], dq, scale, scale2, False)
    total = last.astype(jnp.float32) + up.astype(jnp.float32) + down.astype(jnp.float32)
    half = total.shape[1] // 2
    keep = lax.dynamic_slice_in_dim(total, x * half, half, 1)
    send = lax.dynamic_slice_in_dim(total, (1 - x) * half, half, 1).astype(jnp.bfloat16)
    summed = (keep + x_swap(send).astype(jnp.float32)).astype(jnp.bfloat16)
    dq, (own_grad,) = backward(scal, q, g, stats, (None,), [own], dq, scale, scale2, True)

    beside = lax.ppermute(summed, "tensor", swap(8))
    rows = jnp.concatenate([summed[0], summed[1], beside[0], beside[1]], 1)
    weights = jnp.concatenate([mine[0], mine[1], other[0], other[1]], 2)
    shares = lax.dot_general(
        rows, weights.reshape(4 * cols, 4 * dh), LAST, preferred_element_type=jnp.float32
    ).astype(jnp.bfloat16)

    def share(k):
        return lax.dynamic_slice_in_dim(shares, lax.rem(y + k, 4) * cols, cols, 1)

    result = share(0).astype(jnp.float32)
    for k in (1, 2, 3):
        result = result + lax.ppermute(share(k), "tensor", ring(8, k, 2)).astype(jnp.float32)
    return dq[None], own_grad[None], result.astype(jnp.bfloat16)


def solution(mesh):
    in_specs = (
        P(("prompt", "group"), None, "tensor"),
        P(("prompt", "group"), None, None, "tensor"),
        P(("prompt", "group"), None, "tensor"),
        P(("prompt", "group"), None, None, "tensor"),
        P(None, None, "tensor"),
        P(("prompt", "group")),
        P("prompt"),
        P("prompt"),
    )
    out_specs = (
        P(("prompt", "group"), None, "tensor"),
        P(("prompt", "group"), None, None, "tensor"),
        P(("prompt", "group"), "tensor"),
    )
    return jax.shard_map(
        on_device, mesh=mesh, in_specs=in_specs, out_specs=out_specs, check_vma=False
    )
```

time: 487 us -> 147 us (0.30)
  waiting for transfers between devices: 395 us -> 28 us
  starting transfers between devices: 0.12 us -> 54.5 us
  Pallas kernels: 0 us -> 45.8 us
  matrix products: 34.9 us -> 0.99 us
  other arithmetic: 25.4 us -> 7.5 us
  between operations: 15.3 us -> 3.09 us
  local copies, waits for them, and re-layouts: 13.5 us -> 7.18 us
    reduce_scatter x2 -> x0, waiting for transfers between devices: 241 us -> none  [the longest x1 208 us: on_device(): lax.psum_scatter(jnp.stack([prefix_keys, prefix_values]), 'group', scatte...]
    psum x1 -> x0, waiting for transfers between devices: 154 us -> none  [broadcast(): return lax.psum(block, axis)]
    ppermute x0 -> x28, starting transfers between devices: none -> 54.5 us  [the longest x21 27.6 us: z_hop(): return lax.ppermute(x, 'group', ring(2 * SPLIT, step, 2))]
    pallas_call x0 -> x12, Pallas kernels: none -> 45.8 us  [the longest x6 30.2 us: backward(): pl.pallas_call(functools.partial(backward_kernel, kinds, scale, scale2, f...]
    dot_general x26 -> x1, matrix products: 34.9 us -> 0.99 us  [on_device(): lax.dot_general(rows, weights.reshape(4 * cols, 4 * dh), LAST, preferred_...]
    ppermute x0 -> x28, waiting for transfers between devices: none -> 28 us  [the longest x21 24 us: z_hop(): return lax.ppermute(x, 'group', ring(2 * SPLIT, step, 2))]
    select_n x2 -> x6, other arithmetic: 13.5 us -> 4.84 us  [the longest x2 1.98 us: scatter_prefix(): down = z_hop(own if down is None else jnp.where(is_owner, own, down), -1)]
    reduce_sum x4 -> x0, other arithmetic: 5.84 us -> none  [per_block(): probs = raised / jnp.sum(raised, -1, keepdims=True)]
  transfers between devices with their start and end apart: 3 -> 28, of which waited for: 3 -> 12; matrix products, arithmetic and copies ran while one was open for 1% -> 6% of each run, Pallas kernels for 0% -> 31%
where the time goes in v1:
time: 147 us
  starting transfers between devices  54.5 us (37%)
  Pallas kernels  45.8 us (31%)
  waiting for transfers between devices  28 us (19%)
  other arithmetic  7.5 us (5%)
  local copies, waits for them, and re-layouts  7.18 us (5%)
  between operations  3.09 us (2%)
    pallas_call x6, Pallas kernels, backward(): pl.pallas_call(functools.partial(backward_kernel, kinds, scale, scale2, f...  30.2 us
    ppermute x21, starting transfers between devices, z_hop(): return lax.ppermute(x, 'group', ring(2 * SPLIT, step, 2))  27.6 us
    ppermute x21, waiting for transfers between devices, z_hop(): return lax.ppermute(x, 'group', ring(2 * SPLIT, step, 2))  24 us
    pallas_call x6, Pallas kernels, forward(): pl.pallas_call(functools.partial(forward_kernel, kinds, scale2, first, la...  15.6 us
    ppermute x1, starting transfers between devices, on_device(): lax.ppermute(lax.dynamic_index_in_dim(by_core, 1 - core, 2, keepdims=Fals...  8.48 us
    ppermute x1, starting transfers between devices, on_device(): beside = lax.ppermute(summed, 'tensor', swap(8))  7.73 us
    ppermute x2, starting transfers between devices, x_swap(): return lax.ppermute(x, 'group', swap(2 * SPLIT))  5.67 us
    ppermute x3, starting transfers between devices, on_device(): lax.ppermute(share(k), 'tensor', ring(8, k, 2)).astype(jnp.float32)  5.07 us
  transfers between devices with their start and end apart: 28, of which 12 were waited for; matrix products, arithmetic and copies ran while one was open for 6% of the time, Pallas kernels for 31%

profile of v1, /device:TPU:1, one launch (start us, length us, event | category | flops | bytes accessed | tf_op | source)
XLA Modules:
  0.0 147.1 jit_solution(10779644623990511791)
XLA Ops:
  0.7 1.0 dynamic-slice_bitcast_fusion.1
  1.7 6.5 %collective-permute-start.4 = (bf16[2,256,128]{2,1,0:T(8,128)(2,1)S(1)}, bf16[2,256,128]{2,1,0:T(8,128)(2,1)S(1)}, u32[]{:S(2)}, u32[]{:S(2)}) collective-permute-start(bf16[2,256,128]{2,1,0:T(8,128)(2,1)S(1)} %get-tuple-element.39), channel_id=1, source_target_pairs={{0,112},{8,120},{16,0},{24,8},{32,16},{40,24},{48,32},{56,40},{64,... | collective-permute-start | bytes 393224 | tf_op jit(solution)/shard_map/ppermute | solution.py:168
  8.8 1.5 %collective-permute-done.4 = bf16[2,256,128]{2,1,0:T(8,128)(2,1)S(1)} collective-permute-done((bf16[2,256,128]{2,1,0:T(8,128)(2,1)S(1)}, bf16[2,256,128]{2,1,0:T(8,128)(2,1)S(1)}, u32[]{:S(2)}, u32[]{:S(2)}) %collective-permute-start.4) | collective-permute-done | bytes 131104 | tf_op jit(solution)/shard_map/ppermute | solution.py:168
  11.3 3.5 %collective-permute-start.5 = (bf16[2,256,128]{2,1,0:T(8,128)(2,1)S(1)}, bf16[2,256,128]{2,1,0:T(8,128)(2,1)S(1)}, u32[]{:S(2)}, u32[]{:S(2)}) collective-permute-start(bf16[2,256,128]{2,1,0:T(8,128)(2,1)S(1)} %bitcast_select_fusion), channel_id=1, source_target_pairs={{0,112},{8,120},{16,0},{24,8},{32,16},{40,24},{48,32},{56,40},{64,... | collective-permute-start | bytes 393224 | tf_op jit(solution)/shard_map/ppermute | solution.py:168
  14.8 1.9 %collective-permute-done.5 = bf16[2,256,128]{2,1,0:T(8,128)(2,1)S(1)} collective-permute-done((bf16[2,256,128]{2,1,0:T(8,128)(2,1)S(1)}, bf16[2,256,128]{2,1,0:T(8,128)(2,1)S(1)}, u32[]{:S(2)}, u32[]{:S(2)}) %collective-permute-start.5) | collective-permute-done | bytes 131104 | tf_op jit(solution)/shard_map/ppermute | solution.py:168
  16.7 1.0 bitcast_select_fusion.1
  17.9 5.4 %collective-permute-done.1 = bf16[2,256,128]{2,1,0:T(8,128)(2,1)S(1)} collective-permute-done((bf16[2,256,128]{2,1,0:T(8,128)(2,1)S(1)}, bf16[2,256,128]{2,1,0:T(8,128)(2,1)S(1)}, u32[]{:S(2)}, u32[]{:S(2)}) %collective-permute-start.1) | collective-permute-done | bytes 131104 | tf_op jit(solution)/shard_map/ppermute | solution.py:168
  23.3 0.9 bitcast_select_fusion.3
  24.3 2.6 %collective-permute-start.6 = (bf16[2,256,128]{2,1,0:T(8,128)(2,1)S(1)}, bf16[2,256,128]{2,1,0:T(8,128)(2,1)S(1)}, u32[]{:S(2)}, u32[]{:S(2)}) collective-permute-start(bf16[2,256,128]{2,1,0:T(8,128)(2,1)S(1)} %get-tuple-element.37), channel_id=1, source_target_pairs={{0,112},{8,120},{16,0},{24,8},{32,16},{40,24},{48,32},{56,40},{64,... | collective-permute-start | bytes 393224 | tf_op jit(solution)/shard_map/ppermute | solution.py:168
  27.0 2.4 %collective-permute-done.2 = bf16[2,256,128]{2,1,0:T(8,128)(2,1)S(1)} collective-permute-done((bf16[2,256,128]{2,1,0:T(8,128)(2,1)S(1)}, bf16[2,256,128]{2,1,0:T(8,128)(2,1)S(1)}, u32[]{:S(2)}, u32[]{:S(2)}) %collective-permute-start.2) | collective-permute-done | bytes 131104 | tf_op jit(solution)/shard_map/ppermute | solution.py:168
  29.3 0.9 bitcast_select_fusion.4
  30.4 5.0 %collective-permute-done.3 = bf16[2,256,128]{2,1,0:T(8,128)(2,1)S(1)} collective-permute-done((bf16[2,256,128]{2,1,0:T(8,128)(2,1)S(1)}, bf16[2,256,128]{2,1,0:T(8,128)(2,1)S(1)}, u32[]{:S(2)}, u32[]{:S(2)}) %collective-permute-start.3) | collective-permute-done | bytes 131104 | tf_op jit(solution)/shard_map/ppermute | solution.py:168
  35.4 1.0 bitcast_select_fusion.5
  36.3 2.8 %collective-permute-start.7 = (bf16[2,256,128]{2,1,0:T(8,128)(2,1)S(1)}, bf16[2,256,128]{2,1,0:T(8,128)(2,1)S(1)}, u32[]{:S(2)}, u32[]{:S(2)}) collective-permute-start(bf16[2,256,128]{2,1,0:T(8,128)(2,1)S(1)} %bitcast_select_fusion.5), channel_id=1, source_target_pairs={{0,8},{8,0},{16,24},{24,16},{32,40},{40,32},{48,56},{56,48},{64,72... | collective-permute-start | bytes 393224 | tf_op jit(solution)/shard_map/ppermute | solution.py:172
  39.2 2.6 %collective-permute-done.7 = bf16[2,256,128]{2,1,0:T(8,128)(2,1)S(1)} collective-permute-done((bf16[2,256,128]{2,1,0:T(8,128)(2,1)S(1)}, bf16[2,256,128]{2,1,0:T(8,128)(2,1)S(1)}, u32[]{:S(2)}, u32[]{:S(2)}) %collective-permute-start.7) | collective-permute-done | bytes 131104 | tf_op jit(solution)/shard_map/ppermute | solution.py:172
  42.0 1.3 collective-permute-start.8
  43.3 2.4 %collective-permute-done.12.refs_1_.refs_0_ = bf16[2,256,128]{2,1,0:T(8,128)(2,1)S(1)} collective-permute-done((bf16[2,256,128]{2,1,0:T(8,128)(2,1)S(1)}, bf16[2,256,128]{2,1,0:T(8,128)(2,1)S(1)}, u32[]{:S(2)}, u32[]{:S(2)}) %collective-permute-start.12) | collective-permute-done | bytes 131104 | tf_op jit(solution)/shard_map/ppermute | solution.py:168
  45.7 1.7 %collective-permute-start.13 = (bf16[2,256,128]{2,1,0:T(8,128)(2,1)S(1)}, bf16[2,256,128]{2,1,0:T(8,128)(2,1)S(1)}, u32[]{:S(2)}, u32[]{:S(2)}) collective-permute-start(bf16[2,256,128]{2,1,0:T(8,128)(2,1)S(1)} %collective-permute-done.12.refs_1_.refs_0_), channel_id=1, source_target_pairs={{0,112},{8,120},{16,0},{24,8},{32,16},{40,24},{48,32},{56,40},{64,... | collective-permute-start | bytes 393224 | tf_op jit(solution)/shard_map/ppermute | solution.py:168
  47.4 2.5 %dynamic-slice_bitcast_fusion = bf16[2,4,640,128]{3,2,1,0:T(8,128)(2,1)} fusion(bf16[2,4,2,640,128]{4,3,2,1,0:T(8,128)(2,1)} %bitcast.68, s32[]{:T(128)S(6)} %select_n.141), kind=kLoop, calls=%fused_computation.8 | loop fusion | bytes 2621444 | tf_op jit(solution)/shard_map/jit(dynamic_index_in_dim)/squeeze | solution.py:210
  49.9 8.5 %collective-permute-start.24 = (bf16[2,4,640,128]{3,2,1,0:T(8,128)(2,1)}, bf16[2,4,640,128]{3,2,1,0:T(8,128)(2,1)}, u32[]{:S(2)}, u32[]{:S(2)}) collective-permute-start(bf16[2,4,640,128]{3,2,1,0:T(8,128)(2,1)} %dynamic-slice_bitcast_fusion), channel_id=1, source_target_pairs={{0,1},{1,0},{2,3},{3,2},{4,5},{5,4},{6,7},{7,6},{8,9},{9,8},{10,11... | collective-permute-start | bytes 3932168 | tf_op jit(solution)/shard_map/ppermute | solution.py:210
  59.9 2.9 %collective-permute-start.14 = (bf16[2,256,128]{2,1,0:T(8,128)(2,1)S(1)}, bf16[2,256,128]{2,1,0:T(8,128)(2,1)S(1)}, u32[]{:S(2)}, u32[]{:S(2)}) collective-permute-start(bf16[2,256,128]{2,1,0:T(8,128)(2,1)S(1)} %collective-permute-done.13.refs_1_.refs_0_), channel_id=1, source_target_pairs={{0,112},{8,120},{16,0},{24,8},{32,16},{40,24},{48,32},{56,40},{64,... | collective-permute-start | bytes 393224 | tf_op jit(solution)/shard_map/ppermute | solution.py:168
  62.7 2.6 %shard_map.103.refs_1_ = f32[4,8,512]{2,1,0:T(8,128)S(1)} custom-call(s32[4]{0:T(128)S(1)} %pad_add_fusion.scal_ref, bf16[512,512]{1,0:T(8,128)(2,1)S(1)} %bitcast.42, bf16[512,512]{1,0:T(8,128)(2,1)S(1)} %bitcast.54, bf16[2,512,128]{2,1,0:T(8,128)(2,1)S(1)} %bitcast.66), custom_call_target="tpu_custom_call" | custom-call | flops 536870912 | bytes 1048576 | tf_op jit(solution)/shard_map/pallas_call | solution.py:75
  65.3 2.2 %shard_map.104.refs_2_ = f32[4,8,512]{2,1,0:T(8,128)S(1)} custom-call(s32[4]{0:T(128)S(1)} %pad_add_fusion.scal_ref, bf16[512,512]{1,0:T(8,128)(2,1)S(1)} %bitcast.43, bf16[512,512]{1,0:T(8,128)(2,1)S(1)} %bitcast.55, bf16[2,256,128]{2,1,0:T(8,128)(2,1)S(1)} %broadcast_select_fusion.refs_0_, f32[4,8,512]{2,1,0:T(8,128)S(1)} %shard_map.103.refs_1_), custom_call_target="tpu_custom_call" | custom-call | flops 268435456 | bytes 1048576 | tf_op jit(solution)/shard_map/pallas_call | solution.py:75
  67.6 2.9 %shard_map.105.refs_2_ = f32[4,8,512]{2,1,0:T(8,128)S(1)} custom-call(s32[4]{0:T(128)S(1)} %pad_add_fusion.scal_ref, bf16[512,512]{1,0:T(8,128)(2,1)S(1)} %bitcast.44, bf16[512,512]{1,0:T(8,128)(2,1)S(1)} %bitcast.56, bf16[2,256,128]{2,1,0:T(8,128)(2,1)S(1)} %collective-permute-done.8.refs_0_.refs_1_, ...), custom_call_target="tpu_custom_call" | custom-call | flops 536870912 | bytes 1048576 | tf_op jit(solution)/shard_map/pallas_call | solution.py:75
  70.5 2.9 %shard_map.106.refs_2_ = f32[4,8,512]{2,1,0:T(8,128)S(1)} custom-call(s32[4]{0:T(128)S(1)} %pad_add_fusion.scal_ref, bf16[512,512]{1,0:T(8,128)(2,1)S(1)} %bitcast.45, bf16[512,512]{1,0:T(8,128)(2,1)S(1)} %bitcast.57, bf16[2,256,128]{2,1,0:T(8,128)(2,1)S(1)} %collective-permute-done.9.refs_0_.refs_1_, ...), custom_call_target="tpu_custom_call" | custom-call | flops 536870912 | bytes 1048576 | tf_op jit(solution)/shard_map/pallas_call | solution.py:75
  73.4 2.9 %shard_map.107.refs_1_ = f32[4,8,512]{2,1,0:T(8,128)S(1)} custom-call(s32[4]{0:T(128)S(1)} %pad_add_fusion.scal_ref, bf16[512,512]{1,0:T(8,128)(2,1)S(1)} %bitcast.46, bf16[512,512]{1,0:T(8,128)(2,1)S(1)} %bitcast.58, bf16[2,256,128]{2,1,0:T(8,128)(2,1)S(1)} %collective-permute-done.10.refs_0_.refs_1_, ...), custom_call_target="tpu_custom_call" | custom-call | flops 536870912 | bytes 1048576 | tf_op jit(solution)/shard_map/pallas_call | solution.py:75
  76.3 2.2 %shard_map.108.stat_ref = f32[4,8,512]{2,1,0:T(8,128)S(1)} custom-call(s32[4]{0:T(128)S(1)} %pad_add_fusion.scal_ref, bf16[512,512]{1,0:T(8,128)(2,1)S(1)} %bitcast.47, bf16[512,512]{1,0:T(8,128)(2,1)S(1)} %bitcast.59, bf16[2,256,128]{2,1,0:T(8,128)(2,1)S(1)} %collective-permute-done.11.refs_0_, f32[4,8,512]{2,1,0:T(8,128)S(1)} %shard_map.107.refs_1_), custom_call_target="tpu_custom_call" | custom-call | flops 268435456 | bytes 1048576 | tf_op jit(solution)/shard_map/pallas_call | solution.py:75
  78.6 3.5 %shard_map.109 = (f32[512,512]{1,0:T(8,128)S(1)}, bf16[2,256,128]{2,1,0:T(8,128)(2,1)S(1)}) custom-call(s32[4]{0:T(128)S(1)} %pad_add_fusion.scal_ref, bf16[512,512]{1,0:T(8,128)(2,1)S(1)} %bitcast.48, bf16[512,512]{1,0:T(8,128)(2,1)S(1)} %bitcast.60, f32[4,8,512]{2,1,0:T(8,128)S(1)} %shard_map.108.stat_ref, ...), custom_call_target="tpu_custom_call" | custom-call | flops 671088640 | bytes 1048576 | tf_op jit(solution)/shard_map/pallas_call | solution.py:145
  82.2 5.7 %shard_map.110 = (f32[512,512]{1,0:T(8,128)S(1)}, bf16[2,256,128]{2,1,0:T(8,128)(2,1)S(1)}, bf16[2,256,128]{2,1,0:T(8,128)(2,1)S(1)}) custom-call(s32[4]{0:T(128)S(1)} %pad_add_fusion.scal_ref, bf16[512,512]{1,0:T(8,128)(2,1)S(1)} %bitcast.49, bf16[512,512]{1,0:T(8,128)(2,1)S(1)} %bitcast.61, f32[4,8,512]{2,1,0:T(8,128)S(1)} %shard_map.108.stat_ref, ...), custom_call_target="tpu_custom_call" | custom-call | flops 1342177280 | bytes 1048576 | tf_op jit(solution)/shard_map/pallas_call | solution.py:145
  87.9 2.7 %collective-permute-start.19 = (bf16[2,256,128]{2,1,0:T(8,128)(2,1)S(1)}, bf16[2,256,128]{2,1,0:T(8,128)(2,1)S(1)}, u32[]{:S(2)}, u32[]{:S(2)}) collective-permute-start(bf16[2,256,128]{2,1,0:T(8,128)(2,1)S(1)} %get-tuple-element.32), channel_id=1, source_target_pairs={{0,112},{8,120},{16,0},{24,8},{32,16},{40,24},{48,32},{56,40},{64,... | collective-permute-start | bytes 393224 | tf_op jit(solution)/shard_map/ppermute | solution.py:168
  90.6 5.7 %shard_map.111 = (f32[512,512]{1,0:T(8,128)S(1)}, bf16[2,256,128]{2,1,0:T(8,128)(2,1)S(1)}, bf16[2,256,128]{2,1,0:T(8,128)(2,1)S(1)}) custom-call(s32[4]{0:T(128)S(1)} %pad_add_fusion.scal_ref, bf16[512,512]{1,0:T(8,128)(2,1)S(1)} %bitcast.50, bf16[512,512]{1,0:T(8,128)(2,1)S(1)} %bitcast.62, f32[4,8,512]{2,1,0:T(8,128)S(1)} %shard_map.108.stat_ref, ...), custom_call_target="tpu_custom_call" | custom-call | flops 1342177280 | bytes 1048576 | tf_op jit(solution)/shard_map/pallas_call | solution.py:145
  96.3 5.7 %shard_map.112 = (f32[512,512]{1,0:T(8,128)S(1)}, bf16[2,256,128]{2,1,0:T(8,128)(2,1)S(1)}, bf16[2,256,128]{2,1,0:T(8,128)(2,1)S(1)}) custom-call(s32[4]{0:T(128)S(1)} %pad_add_fusion.scal_ref, bf16[512,512]{1,0:T(8,128)(2,1)S(1)} %bitcast.51, bf16[512,512]{1,0:T(8,128)(2,1)S(1)} %bitcast.63, f32[4,8,512]{2,1,0:T(8,128)S(1)} %shard_map.108.stat_ref, ...), custom_call_target="tpu_custom_call" | custom-call | flops 1342177280 | bytes 1048576 | tf_op jit(solution)/shard_map/pallas_call | solution.py:145
  102.2 2.7 %collective-permute-start.20 = (bf16[2,256,128]{2,1,0:T(8,128)(2,1)S(1)}, bf16[2,256,128]{2,1,0:T(8,128)(2,1)S(1)}, u32[]{:S(2)}, u32[]{:S(2)}) collective-permute-start(bf16[2,256,128]{2,1,0:T(8,128)(2,1)S(1)} %add_convert_fusion.2), channel_id=1, source_target_pairs={{0,112},{8,120},{16,0},{24,8},{32,16},{40,24},{48,32},{56,40},{64,... | collective-permute-start | bytes 393224 | tf_op jit(solution)/shard_map/ppermute | solution.py:168
  104.9 2.2 %collective-permute-done.16 = bf16[2,256,128]{2,1,0:T(8,128)(2,1)S(1)} collective-permute-done((bf16[2,256,128]{2,1,0:T(8,128)(2,1)S(1)}, bf16[2,256,128]{2,1,0:T(8,128)(2,1)S(1)}, u32[]{:S(2)}, u32[]{:S(2)}) %collective-permute-start.16) | collective-permute-done | bytes 131104 | tf_op jit(solution)/shard_map/ppermute | solution.py:168
  107.4 2.7 %collective-permute-start.21 = (bf16[2,256,128]{2,1,0:T(8,128)(2,1)S(1)}, bf16[2,256,128]{2,1,0:T(8,128)(2,1)S(1)}, u32[]{:S(2)}, u32[]{:S(2)}) collective-permute-start(bf16[2,256,128]{2,1,0:T(8,128)(2,1)S(1)} %add_convert_fusion.1), channel_id=1, source_target_pairs={{0,112},{8,120},{16,0},{24,8},{32,16},{40,24},{48,32},{56,40},{64,... | collective-permute-start | bytes 393224 | tf_op jit(solution)/shard_map/ppermute | solution.py:168
  110.1 2.2 %collective-permute-done.17 = bf16[2,256,128]{2,1,0:T(8,128)(2,1)S(1)} collective-permute-done((bf16[2,256,128]{2,1,0:T(8,128)(2,1)S(1)}, bf16[2,256,128]{2,1,0:T(8,128)(2,1)S(1)}, u32[]{:S(2)}, u32[]{:S(2)}) %collective-permute-start.17) | collective-permute-done | bytes 131104 | tf_op jit(solution)/shard_map/ppermute | solution.py:168
  114.0 3.6 %shard_map.113 = (f32[512,512]{1,0:T(8,128)S(1)}, bf16[2,256,128]{2,1,0:T(8,128)(2,1)S(1)}) custom-call(s32[4]{0:T(128)S(1)} %pad_add_fusion.scal_ref, bf16[512,512]{1,0:T(8,128)(2,1)S(1)} %bitcast.52, bf16[512,512]{1,0:T(8,128)(2,1)S(1)} %bitcast.64, f32[4,8,512]{2,1,0:T(8,128)S(1)} %shard_map.108.stat_ref, ...), custom_call_target="tpu_custom_call" | custom-call | flops 671088640 | bytes 1048576 | tf_op jit(solution)/shard_map/pallas_call | solution.py:145
  117.5 1.0 collective-permute-done.18
  118.5 1.0 convert_add_fusion
  119.5 2.8 %collective-permute-start.22 = (bf16[2,128,128]{2,1,0:T(8,128)(2,1)S(1)}, bf16[2,128,128]{2,1,0:T(8,128)(2,1)S(1)}, u32[]{:S(2)}, u32[]{:S(2)}) collective-permute-start(bf16[2,128,128]{2,1,0:T(8,128)(2,1)S(1)} %dynamic-slice_convert_fusion), channel_id=1, source_target_pairs={{0,8},{8,0},{16,24},{24,16},{32,40},{40,32},{48,56},{56,48},{64,72... | collective-permute-start | bytes 196616 | tf_op jit(solution)/shard_map/ppermute | solution.py:172
  122.4 1.4 fusion.15
  124.2 7.7 %collective-permute-start.23 = (bf16[2,128,128]{2,1,0:T(8,128)(2,1)S(1)}, bf16[2,128,128]{2,1,0:T(8,128)(2,1)S(1)}, u32[]{:S(2)}, u32[]{:S(2)}) collective-permute-start(bf16[2,128,128]{2,1,0:T(8,128)(2,1)S(1)} %add_convert_fusion.6), channel_id=1, source_target_pairs={{0,1},{1,0},{2,3},{3,2},{4,5},{5,4},{6,7},{7,6},{8,9},{9,8},{10,11... | collective-permute-start | bytes 196616 | tf_op jit(solution)/shard_map/ppermute | solution.py:245
  132.9 1.0 convolution_convert_fusion
  134.0 1.4 collective-permute-start.25
  135.3 2.6 %collective-permute-start.26 = (bf16[128,640]{1,0:T(8,128)(2,1)S(1)}, bf16[128,640]{1,0:T(8,128)(2,1)S(1)}, u32[]{:S(2)}, u32[]{:S(2)}) collective-permute-start(bf16[128,640]{1,0:T(8,128)(2,1)S(1)} %get-tuple-element.43), channel_id=1, source_target_pairs={{0,4},{1,5},{2,6},{3,7},{4,0},{5,1},{6,2},{7,3},{8,12},{9,13},{10,... | collective-permute-start | bytes 491528 | tf_op jit(solution)/shard_map/ppermute | solution.py:257
  138.0 1.1 collective-permute-start.27
  139.0 1.2 copy-done.4
  140.3 6.0 %shard_map.114 = (bf16[512,512]{1,0:T(8,128)(2,1)}, bf16[2,512,128]{2,1,0:T(8,128)(2,1)}) custom-call(s32[4]{0:T(128)S(1)} %pad_add_fusion.scal_ref, bf16[512,512]{1,0:T(8,128)(2,1)S(1)} %bitcast.53, bf16[512,512]{1,0:T(8,128)(2,1)S(1)} %bitcast.65, f32[4,8,512]{2,1,0:T(8,128)S(1)} %shard_map.108.stat_ref, bf16[2,512,128]{2,1,0:T(8,128)(2,1)S(1)} %bitcast.67, ...), custom_call_target="tpu_custom_call" | custom-call | flops 1342177280 | bytes 1048576 | tf_op jit(solution)/shard_map/pallas_call | solution.py:145
  (58 shorter events, 6.1 us)
Async XLA Ops:
  1.7 8.6 %collective-permute-start.4 = (bf16[2,256,128]{2,1,0:T(8,128)(2,1)S(1)}, bf16[2,256,128]{2,1,0:T(8,128)(2,1)S(1)}, u32[]{:S(2)}, u32[]{:S(2)}) collective-permute-start(bf16[2,256,128]{2,1,0:T(8,128)(2,1)S(1)} %get-tuple-element.39), channel_id=1, source_target_pairs={{0,112},{8,120},{16,0},{24,8},{32,16},{40,24},{48,32},{56,40},{64,... | collective-permute-start | bytes 393224 | tf_op jit(solution)/shard_map/ppermute | solution.py:168
  8.2 6.6 %collective-permute-start = (bf16[2,256,128]{2,1,0:T(8,128)(2,1)S(1)}, bf16[2,256,128]{2,1,0:T(8,128)(2,1)S(1)}, u32[]{:S(2)}, u32[]{:S(2)}) collective-permute-start(bf16[2,256,128]{2,1,0:T(8,128)(2,1)S(1)} %get-tuple-element.40), channel_id=1, source_target_pairs={{0,16},{8,24},{16,32},{24,40},{32,48},{40,56},{48,64},{56,72},{64,... | collective-permute-start | bytes 393224 | tf_op jit(solution)/shard_map/ppermute | solution.py:168
  11.3 5.4 %collective-permute-start.5 = (bf16[2,256,128]{2,1,0:T(8,128)(2,1)S(1)}, bf16[2,256,128]{2,1,0:T(8,128)(2,1)S(1)}, u32[]{:S(2)}, u32[]{:S(2)}) collective-permute-start(bf16[2,256,128]{2,1,0:T(8,128)(2,1)S(1)} %bitcast_select_fusion), channel_id=1, source_target_pairs={{0,112},{8,120},{16,0},{24,8},{32,16},{40,24},{48,32},{56,40},{64,... | collective-permute-start | bytes 393224 | tf_op jit(solution)/shard_map/ppermute | solution.py:168
  14.8 48.0 %copy-start = (bf16[1,512,512]{2,1,0:T(8,128)(2,1)S(1)}, bf16[1,512,512]{2,1,0:T(8,128)(2,1)}, u32[]{:S(2)}) copy-start(bf16[1,512,512]{2,1,0:T(8,128)(2,1)} %param.8) | copy-start | bytes 1572868
  14.8 48.0 %copy-start.1 = (bf16[1,512,512]{2,1,0:T(8,128)(2,1)S(1)}, bf16[1,512,512]{2,1,0:T(8,128)(2,1)}, u32[]{:S(2)}) copy-start(bf16[1,512,512]{2,1,0:T(8,128)(2,1)} %param.10) | copy-start | bytes 1572868
  14.8 48.0 %copy-start.2 = (bf16[1,2,512,128]{3,2,1,0:T(8,128)(2,1)S(1)}, bf16[1,2,512,128]{3,2,1,0:T(8,128)(2,1)}, u32[]{:S(2)}) copy-start(bf16[1,2,512,128]{3,2,1,0:T(8,128)(2,1)} %param.9) | copy-start | bytes 786436
  17.7 5.5 %collective-permute-start.1 = (bf16[2,256,128]{2,1,0:T(8,128)(2,1)S(1)}, bf16[2,256,128]{2,1,0:T(8,128)(2,1)S(1)}, u32[]{:S(2)}, u32[]{:S(2)}) collective-permute-start(bf16[2,256,128]{2,1,0:T(8,128)(2,1)S(1)} %get-tuple-element.38), channel_id=1, source_target_pairs={{0,16},{8,24},{16,32},{24,40},{32,48},{40,56},{48,64},{56,72},{64,... | collective-permute-start | bytes 393224 | tf_op jit(solution)/shard_map/ppermute | solution.py:168
  24.2 5.1 %collective-permute-start.2 = (bf16[2,256,128]{2,1,0:T(8,128)(2,1)S(1)}, bf16[2,256,128]{2,1,0:T(8,128)(2,1)S(1)}, u32[]{:S(2)}, u32[]{:S(2)}) collective-permute-start(bf16[2,256,128]{2,1,0:T(8,128)(2,1)S(1)} %bitcast_select_fusion.3), channel_id=1, source_target_pairs={{0,16},{8,24},{16,32},{24,40},{32,48},{40,56},{48,64},{56,72},{64,... | collective-permute-start | bytes 393224 | tf_op jit(solution)/shard_map/ppermute | solution.py:168
  24.3 6.1 %collective-permute-start.6 = (bf16[2,256,128]{2,1,0:T(8,128)(2,1)S(1)}, bf16[2,256,128]{2,1,0:T(8,128)(2,1)S(1)}, u32[]{:S(2)}, u32[]{:S(2)}) collective-permute-start(bf16[2,256,128]{2,1,0:T(8,128)(2,1)S(1)} %get-tuple-element.37), channel_id=1, source_target_pairs={{0,112},{8,120},{16,0},{24,8},{32,16},{40,24},{48,32},{56,40},{64,... | collective-permute-start | bytes 393224 | tf_op jit(solution)/shard_map/ppermute | solution.py:168
  30.3 5.1 %collective-permute-start.3 = (bf16[2,256,128]{2,1,0:T(8,128)(2,1)S(1)}, bf16[2,256,128]{2,1,0:T(8,128)(2,1)S(1)}, u32[]{:S(2)}, u32[]{:S(2)}) collective-permute-start(bf16[2,256,128]{2,1,0:T(8,128)(2,1)S(1)} %bitcast_select_fusion.4), channel_id=1, source_target_pairs={{0,16},{8,24},{16,32},{24,40},{32,48},{40,56},{48,64},{56,72},{64,... | collective-permute-start | bytes 393224 | tf_op jit(solution)/shard_map/ppermute | solution.py:168
  36.3 5.4 %collective-permute-start.7 = (bf16[2,256,128]{2,1,0:T(8,128)(2,1)S(1)}, bf16[2,256,128]{2,1,0:T(8,128)(2,1)S(1)}, u32[]{:S(2)}, u32[]{:S(2)}) collective-permute-start(bf16[2,256,128]{2,1,0:T(8,128)(2,1)S(1)} %bitcast_select_fusion.5), channel_id=1, source_target_pairs={{0,8},{8,0},{16,24},{24,16},{32,40},{40,32},{48,56},{56,48},{64,72... | collective-permute-start | bytes 393224 | tf_op jit(solution)/shard_map/ppermute | solution.py:172
  41.8 3.9 %collective-permute-start.12 = (bf16[2,256,128]{2,1,0:T(8,128)(2,1)S(1)}, bf16[2,256,128]{2,1,0:T(8,128)(2,1)S(1)}, u32[]{:S(2)}, u32[]{:S(2)}) collective-permute-start(bf16[2,256,128]{2,1,0:T(8,128)(2,1)S(1)} %broadcast_select_fusion.refs_0_), channel_id=1, source_target_pairs={{0,112},{8,120},{16,0},{24,8},{32,16},{40,24},{48,32},{56,40},{64,... | collective-permute-start | bytes 393224 | tf_op jit(solution)/shard_map/ppermute | solution.py:168
  42.0 5.3 %collective-permute-start.8 = (bf16[2,256,128]{2,1,0:T(8,128)(2,1)S(1)}, bf16[2,256,128]{2,1,0:T(8,128)(2,1)S(1)}, u32[]{:S(2)}, u32[]{:S(2)}) collective-permute-start(bf16[2,256,128]{2,1,0:T(8,128)(2,1)S(1)} %broadcast_select_fusion.refs_0_), channel_id=1, source_target_pairs={{0,16},{8,24},{16,32},{24,40},{32,48},{40,56},{48,64},{56,72},{64,... | collective-permute-start | bytes 393224 | tf_op jit(solution)/shard_map/ppermute | solution.py:168
  45.7 14.2 %collective-permute-start.13 = (bf16[2,256,128]{2,1,0:T(8,128)(2,1)S(1)}, bf16[2,256,128]{2,1,0:T(8,128)(2,1)S(1)}, u32[]{:S(2)}, u32[]{:S(2)}) collective-permute-start(bf16[2,256,128]{2,1,0:T(8,128)(2,1)S(1)} %collective-permute-done.12.refs_1_.refs_0_), channel_id=1, source_target_pairs={{0,112},{8,120},{16,0},{24,8},{32,16},{40,24},{48,32},{56,40},{64,... | collective-permute-start | bytes 393224 | tf_op jit(solution)/shard_map/ppermute | solution.py:168
  47.4 12.3 %collective-permute-start.9 = (bf16[2,256,128]{2,1,0:T(8,128)(2,1)S(1)}, bf16[2,256,128]{2,1,0:T(8,128)(2,1)S(1)}, u32[]{:S(2)}, u32[]{:S(2)}) collective-permute-start(bf16[2,256,128]{2,1,0:T(8,128)(2,1)S(1)} %collective-permute-done.8.refs_0_.refs_1_), channel_id=1, source_target_pairs={{0,16},{8,24},{16,32},{24,40},{32,48},{40,56},{48,64},{56,72},{64,... | collective-permute-start | bytes 393224 | tf_op jit(solution)/shard_map/ppermute | solution.py:168
  49.9 72.5 %collective-permute-start.24 = (bf16[2,4,640,128]{3,2,1,0:T(8,128)(2,1)}, bf16[2,4,640,128]{3,2,1,0:T(8,128)(2,1)}, u32[]{:S(2)}, u32[]{:S(2)}) collective-permute-start(bf16[2,4,640,128]{3,2,1,0:T(8,128)(2,1)} %dynamic-slice_bitcast_fusion), channel_id=1, source_target_pairs={{0,1},{1,0},{2,3},{3,2},{4,5},{5,4},{6,7},{7,6},{8,9},{9,8},{10,11... | collective-permute-start | bytes 3932168 | tf_op jit(solution)/shard_map/ppermute | solution.py:210
  59.7 7.9 %collective-permute-start.10 = (bf16[2,256,128]{2,1,0:T(8,128)(2,1)S(1)}, bf16[2,256,128]{2,1,0:T(8,128)(2,1)S(1)}, u32[]{:S(2)}, u32[]{:S(2)}) collective-permute-start(bf16[2,256,128]{2,1,0:T(8,128)(2,1)S(1)} %collective-permute-done.9.refs_0_.refs_1_), channel_id=1, source_target_pairs={{0,16},{8,24},{16,32},{24,40},{32,48},{40,56},{48,64},{56,72},{64,... | collective-permute-start | bytes 393224 | tf_op jit(solution)/shard_map/ppermute | solution.py:168
  59.9 13.6 %collective-permute-start.14 = (bf16[2,256,128]{2,1,0:T(8,128)(2,1)S(1)}, bf16[2,256,128]{2,1,0:T(8,128)(2,1)S(1)}, u32[]{:S(2)}, u32[]{:S(2)}) collective-permute-start(bf16[2,256,128]{2,1,0:T(8,128)(2,1)S(1)} %collective-permute-done.13.refs_1_.refs_0_), channel_id=1, source_target_pairs={{0,112},{8,120},{16,0},{24,8},{32,16},{40,24},{48,32},{56,40},{64,... | collective-permute-start | bytes 393224 | tf_op jit(solution)/shard_map/ppermute | solution.py:168
  67.5 8.8 %collective-permute-start.11 = (bf16[2,256,128]{2,1,0:T(8,128)(2,1)S(1)}, bf16[2,256,128]{2,1,0:T(8,128)(2,1)S(1)}, u32[]{:S(2)}, u32[]{:S(2)}) collective-permute-start(bf16[2,256,128]{2,1,0:T(8,128)(2,1)S(1)} %collective-permute-done.10.refs_0_.refs_1_), channel_id=1, source_target_pairs={{0,16},{8,24},{16,32},{24,40},{32,48},{40,56},{48,64},{56,72},{64,... | collective-permute-start | bytes 393224 | tf_op jit(solution)/shard_map/ppermute | solution.py:168
  82.1 20.0 %collective-permute-start.15 = (bf16[2,256,128]{2,1,0:T(8,128)(2,1)S(1)}, bf16[2,256,128]{2,1,0:T(8,128)(2,1)S(1)}, u32[]{:S(2)}, u32[]{:S(2)}) collective-permute-start(bf16[2,256,128]{2,1,0:T(8,128)(2,1)S(1)} %get-tuple-element.29), channel_id=1, source_target_pairs={{0,16},{8,24},{16,32},{24,40},{32,48},{40,56},{48,64},{56,72},{64,... | collective-permute-start | bytes 393224 | tf_op jit(solution)/shard_map/ppermute | solution.py:168
  87.9 14.3 %collective-permute-start.19 = (bf16[2,256,128]{2,1,0:T(8,128)(2,1)S(1)}, bf16[2,256,128]{2,1,0:T(8,128)(2,1)S(1)}, u32[]{:S(2)}, u32[]{:S(2)}) collective-permute-start(bf16[2,256,128]{2,1,0:T(8,128)(2,1)S(1)} %get-tuple-element.32), channel_id=1, source_target_pairs={{0,112},{8,120},{16,0},{24,8},{32,16},{40,24},{48,32},{56,40},{64,... | collective-permute-start | bytes 393224 | tf_op jit(solution)/shard_map/ppermute | solution.py:168
  96.3 16.7 %copy-start.5 = (bf16[2,5120,128]{2,1,0:T(8,128)(2,1)S(1)}, bf16[2,5120,128]{2,1,0:T(8,128)(2,1)}, u32[]{:S(2)}) copy-start(bf16[2,5120,128]{2,1,0:T(8,128)(2,1)} %param.12) | copy-start | bytes 7864324
  102.1 5.1 %collective-permute-start.16 = (bf16[2,256,128]{2,1,0:T(8,128)(2,1)S(1)}, bf16[2,256,128]{2,1,0:T(8,128)(2,1)S(1)}, u32[]{:S(2)}, u32[]{:S(2)}) collective-permute-start(bf16[2,256,128]{2,1,0:T(8,128)(2,1)S(1)} %add_convert_fusion.5), channel_id=1, source_target_pairs={{0,16},{8,24},{16,32},{24,40},{32,48},{40,56},{48,64},{56,72},{64,... | collective-permute-start | bytes 393224 | tf_op jit(solution)/shard_map/ppermute | solution.py:168
  102.2 5.1 %collective-permute-start.20 = (bf16[2,256,128]{2,1,0:T(8,128)(2,1)S(1)}, bf16[2,256,128]{2,1,0:T(8,128)(2,1)S(1)}, u32[]{:S(2)}, u32[]{:S(2)}) collective-permute-start(bf16[2,256,128]{2,1,0:T(8,128)(2,1)S(1)} %add_convert_fusion.2), channel_id=1, source_target_pairs={{0,112},{8,120},{16,0},{24,8},{32,16},{40,24},{48,32},{56,40},{64,... | collective-permute-start | bytes 393224 | tf_op jit(solution)/shard_map/ppermute | solution.py:168
  107.2 5.1 %collective-permute-start.17 = (bf16[2,256,128]{2,1,0:T(8,128)(2,1)S(1)}, bf16[2,256,128]{2,1,0:T(8,128)(2,1)S(1)}, u32[]{:S(2)}, u32[]{:S(2)}) collective-permute-start(bf16[2,256,128]{2,1,0:T(8,128)(2,1)S(1)} %add_convert_fusion.4), channel_id=1, source_target_pairs={{0,16},{8,24},{16,32},{24,40},{32,48},{40,56},{48,64},{56,72},{64,... | collective-permute-start | bytes 393224 | tf_op jit(solution)/shard_map/ppermute | solution.py:168
  107.4 10.2 %collective-permute-start.21 = (bf16[2,256,128]{2,1,0:T(8,128)(2,1)S(1)}, bf16[2,256,128]{2,1,0:T(8,128)(2,1)S(1)}, u32[]{:S(2)}, u32[]{:S(2)}) collective-permute-start(bf16[2,256,128]{2,1,0:T(8,128)(2,1)S(1)} %add_convert_fusion.1), channel_id=1, source_target_pairs={{0,112},{8,120},{16,0},{24,8},{32,16},{40,24},{48,32},{56,40},{64,... | collective-permute-start | bytes 393224 | tf_op jit(solution)/shard_map/ppermute | solution.py:168
  113.0 5.5 %collective-permute-start.18 = (bf16[2,256,128]{2,1,0:T(8,128)(2,1)}, bf16[2,256,128]{2,1,0:T(8,128)(2,1)}, u32[]{:S(2)}, u32[]{:S(2)}) collective-permute-start(bf16[2,256,128]{2,1,0:T(8,128)(2,1)} %add_convert_fusion.3), channel_id=1, source_target_pairs={{0,16},{8,24},{16,32},{24,40},{32,48},{40,56},{48,64},{56,72},{64,... | collective-permute-start | bytes 393224 | tf_op jit(solution)/shard_map/ppermute | solution.py:168
  114.0 18.9 %copy-start.6 = (bf16[1,4,1,640,128]{4,3,2,1,0:T(8,128)(2,1)S(1)}, bf16[1,4,1,640,128]{4,3,2,1,0:T(8,128)(2,1)}, u32[]{:S(2)}) copy-start(bf16[1,4,1,640,128]{4,3,2,1,0:T(8,128)(2,1)} %get-tuple-element.34) | copy-start | bytes 1966084
  117.5 16.4 %copy-start.3 = (f32[512,512]{1,0:T(8,128)}, f32[512,512]{1,0:T(8,128)S(1)}, u32[]{:S(2)}) copy-start(f32[512,512]{1,0:T(8,128)S(1)} %get-tuple-element.22.refs_1_) | copy-start | bytes 3145732
  119.5 4.7 %collective-permute-start.22 = (bf16[2,128,128]{2,1,0:T(8,128)(2,1)S(1)}, bf16[2,128,128]{2,1,0:T(8,128)(2,1)S(1)}, u32[]{:S(2)}, u32[]{:S(2)}) collective-permute-start(bf16[2,128,128]{2,1,0:T(8,128)(2,1)S(1)} %dynamic-slice_convert_fusion), channel_id=1, source_target_pairs={{0,8},{8,0},{16,24},{24,16},{32,40},{40,32},{48,56},{56,48},{64,72... | collective-permute-start | bytes 196616 | tf_op jit(solution)/shard_map/ppermute | solution.py:172
  124.2 8.6 %collective-permute-start.23 = (bf16[2,128,128]{2,1,0:T(8,128)(2,1)S(1)}, bf16[2,128,128]{2,1,0:T(8,128)(2,1)S(1)}, u32[]{:S(2)}, u32[]{:S(2)}) collective-permute-start(bf16[2,128,128]{2,1,0:T(8,128)(2,1)S(1)} %add_convert_fusion.6), channel_id=1, source_target_pairs={{0,1},{1,0},{2,3},{3,2},{4,5},{5,4},{6,7},{7,6},{8,9},{9,8},{10,11... | collective-permute-start | bytes 196616 | tf_op jit(solution)/shard_map/ppermute | solution.py:245
  134.0 12.3 %collective-permute-start.25 = (bf16[128,640]{1,0:T(8,128)(2,1)S(1)}, bf16[128,640]{1,0:T(8,128)(2,1)S(1)}, u32[]{:S(2)}, u32[]{:S(2)}) collective-permute-start(bf16[128,640]{1,0:T(8,128)(2,1)S(1)} %get-tuple-element.41), channel_id=1, source_target_pairs={{0,2},{1,3},{2,4},{3,5},{4,6},{5,7},{6,0},{7,1},{8,10},{9,11},{10,... | collective-permute-start | bytes 491528 | tf_op jit(solution)/shard_map/ppermute | solution.py:257
  135.3 11.0 %collective-permute-start.26 = (bf16[128,640]{1,0:T(8,128)(2,1)S(1)}, bf16[128,640]{1,0:T(8,128)(2,1)S(1)}, u32[]{:S(2)}, u32[]{:S(2)}) collective-permute-start(bf16[128,640]{1,0:T(8,128)(2,1)S(1)} %get-tuple-element.43), channel_id=1, source_target_pairs={{0,4},{1,5},{2,6},{3,7},{4,0},{5,1},{6,2},{7,3},{8,12},{9,13},{10,... | collective-permute-start | bytes 491528 | tf_op jit(solution)/shard_map/ppermute | solution.py:257
  138.0 8.3 %collective-permute-start.27 = (bf16[128,640]{1,0:T(8,128)(2,1)S(1)}, bf16[128,640]{1,0:T(8,128)(2,1)S(1)}, u32[]{:S(2)}, u32[]{:S(2)}) collective-permute-start(bf16[128,640]{1,0:T(8,128)(2,1)S(1)} %get-tuple-element.42), channel_id=1, source_target_pairs={{0,6},{1,7},{2,0},{3,1},{4,2},{5,3},{6,4},{7,5},{8,14},{9,15},{10,... | collective-permute-start | bytes 491528 | tf_op jit(solution)/shard_map/ppermute | solution.py:257
  139.0 1.2 copy-start.4

commit v2 on v1

--- a/solution.py
+++ b/solution.py
@@ -172,22 +172,8 @@
     return lax.ppermute(x, "group", swap(2 * SPLIT))
 
 
-def scatter_prefix(prefix, z, owner_z):
-    keys = prefix.shape[1] // SPLIT
-    is_owner = z == owner_z
-
-    def piece(step):
-        return lax.dynamic_slice_in_dim(prefix, lax.rem(z + step + SPLIT, SPLIT) * keys, keys, 1)
-
-    up = down = None
-    for left in range(SPLIT // 2, 0, -1):
-        own = piece(left)
-        up = z_hop(own if up is None else jnp.where(is_owner, own, up), 1)
-        if left < SPLIT // 2:
-            own = piece(-left)
-            down = z_hop(own if down is None else jnp.where(is_owner, own, down), -1)
-    away = lax.rem(z - owner_z + SPLIT, SPLIT)
-    return jnp.where(is_owner, piece(0), jnp.where(away <= SPLIT // 2, up, down))
+def after(value, *done):
+    return lax.optimization_barrier((value, *done))[0]
 
 
 def add_low(a, b):
@@ -201,53 +187,86 @@
     dh = prefix_kv.shape[3]
     scale = dh ** (-0.5)
     scale2 = scale * LOG2E
-    q, g, own = queries[0], grad_out[0], response_kv[0]
+    q, g, own, prefix = queries[0], grad_out[0], response_kv[0], prefix_kv[0]
     scal = jnp.stack([prefix_len[0], resp_len[0], z, z]).astype(jnp.int32)
+
+    keys = prefix.shape[1] // SPLIT
+    half_way = SPLIT // 2
+    owner_z = owner[0] // 2
+    is_owner = z == owner_z
+    first = lax.dynamic_slice_in_dim(prefix, lax.rem(z + half_way, SPLIT) * keys, keys, 1)
+    turned = lax.dynamic_slice_in_dim(jnp.concatenate([prefix, prefix], 1), z * keys, SPLIT * keys, 1)
+    turned = after(turned)
+
+    def piece(step):
+        return lax.slice_in_dim(turned, step % SPLIT * keys, (step % SPLIT + 1) * keys, axis=1)
 
     cols = kv_weight.shape[1] // 8
     by_core = kv_weight.reshape(2, 4, 2, cols, dh)
     mine = lax.dynamic_index_in_dim(by_core, core, 2, keepdims=False)
-    other = lax.ppermute(lax.dynamic_index_in_dim(by_core, 1 - core, 2, keepdims=False), "tensor", swap(8))
-
+    theirs = lax.dynamic_index_in_dim(by_core, 1 - core, 2, keepdims=False)
+
+    up = z_hop(first, 1)
+    down = z_hop(piece(1 - half_way), -1)
+    theirs = after(theirs, turned)
+    up, down, theirs, mine = lax.optimization_barrier((up, down, theirs, mine))
+    other = lax.ppermute(theirs, "tensor", swap(8))
+    up = z_hop(jnp.where(is_owner, piece(half_way - 1), up), 1)
+    down = z_hop(jnp.where(is_owner, piece(2 - half_way), down), -1)
+    up, down, other = lax.optimization_barrier((up, down, other))
+    weights = jnp.concatenate([mine[0], mine[1], other[0], other[1]], 2).reshape(4 * cols, 4 * dh)
+    up = z_hop(jnp.where(is_owner, piece(half_way - 2), up), 1)
+    down = z_hop(jnp.where(is_owner, piece(3 - half_way), down), -1)
+    up, weights = lax.optimization_barrier((up, weights))
+    up = z_hop(jnp.where(is_owner, piece(half_way - 3), up), 1)
     stats = forward(scal, q, g, (None,), [own], None, scale2, False)
-
-    piece = scatter_prefix(prefix_kv[0], z, owner[0] // 2)
-    piece = jnp.where(x == owner[0] % 2, piece, x_swap(piece))
-
-    pieces = {0: piece}
-    stats = forward(scal, q, g, (0,), [piece], stats, scale2, False)
-    up = down = piece
-    for hop in range(1, SPLIT // 2 + 1):
+    up, stats = lax.optimization_barrier((up, stats))
+    away = lax.rem(z - owner_z + SPLIT, SPLIT)
+    held = jnp.where(is_owner, piece(0), jnp.where(away <= half_way, up, down))
+    held = jnp.where(x == owner[0] % 2, held, x_swap(held))
+
+    pieces = {0: held}
+    new = [0]
+    up = down = held
+    for hop in range(1, half_way + 1):
         up = z_hop(up, 1)
-        pieces[SPLIT - hop] = up
+        if hop < half_way:
+            down = z_hop(down, -1)
+        stats = forward(scal, q, g, tuple(new), [pieces[k] for k in new], stats, scale2, False)
         new = [SPLIT - hop]
-        if hop < SPLIT // 2:
-            down = z_hop(down, -1)
+        if hop < half_way:
+            up, down, stats = lax.optimization_barrier((up, down, stats))
             pieces[hop] = down
             new.append(hop)
-        stats = forward(scal, q, g, tuple(new), [pieces[k] for k in new], stats, scale2, hop == SPLIT // 2)
-
-    dq = up = down = None
-    for left in range(SPLIT // 2, 0, -1):
-        new = [left] if left == SPLIT // 2 else [left, SPLIT - left]
-        dq, grads = backward(scal, q, g, stats, tuple(new), [pieces[k] for k in new], dq, scale, scale2, False)
-        up = z_hop(grads[0] if up is None else add_low(grads[0], up), 1)
-        if len(new) > 1:
-            down = z_hop(grads[1] if down is None else add_low(grads[1], down), -1)
-    dq, (last,) = backward(scal, q, g, stats, (0,), [pieces[0]], dq, scale, scale2, False)
-    total = last.astype(jnp.float32) + up.astype(jnp.float32) + down.astype(jnp.float32)
-    half = total.shape[1] // 2
-    keep = lax.dynamic_slice_in_dim(total, x * half, half, 1)
-    send = lax.dynamic_slice_in_dim(total, (1 - x) * half, half, 1).astype(jnp.bfloat16)
-    summed = (keep + x_swap(send).astype(jnp.float32)).astype(jnp.bfloat16)
+        else:
+            up, stats = lax.optimization_barrier((up, stats))
+        pieces[SPLIT - hop] = up
+    stats = forward(scal, q, g, tuple(new), [pieces[k] for k in new], stats, scale2, True)
+
+    dq, (grad,) = backward(scal, q, g, stats, (half_way,), [pieces[half_way]], None, scale, scale2, False)
+    up, down = z_hop(grad, 1), None
+    for left in range(half_way - 1, 0, -1):
+        new = (left, SPLIT - left)
+        dq, grads = backward(scal, q, g, stats, new, [pieces[k] for k in new], dq, scale, scale2, False)
+        up, dq, *grads = lax.optimization_barrier((up, dq, *grads))
+        up = z_hop(add_low(grads[0], up), 1)
+        down = z_hop(grads[1] if down is None else add_low(grads[1], down), -1)
+    dq, (grad,) = backward(scal, q, g, stats, (0,), [pieces[0]], dq, scale, scale2, False)
+    up, down, dq, grad = lax.optimization_barrier((up, down, dq, grad))
+    half = keys // 2
+
+    def rows_of(at):
+        up_, down_, grad_ = (lax.dynamic_slice_in_dim(v, at * half, half, 1).astype(jnp.float32) for v in (up, down, grad))
+        return up_ + down_ + grad_
+
+    swapped = x_swap(rows_of(1 - x).astype(jnp.bfloat16))
     dq, (own_grad,) = backward(scal, q, g, stats, (None,), [own], dq, scale, scale2, True)
+    swapped, dq, own_grad = lax.optimization_barrier((swapped, dq, own_grad))
+    summed = (rows_of(x) + swapped.astype(jnp.float32)).astype(jnp.bfloat16)
 
     beside = lax.ppermute(summed, "tensor", swap(8))
     rows = jnp.concatenate([summed[0], summed[1], beside[0], beside[1]], 1)
-    weights = jnp.concatenate([mine[0], mine[1], other[0], other[1]], 2)
-    shares = lax.dot_general(
-        rows, weights.reshape(4 * cols, 4 * dh), LAST, preferred_element_type=jnp.float32
-    ).astype(jnp.bfloat16)
+    shares = lax.dot_general(rows, weights, LAST, preferred_element_type=jnp.float32).astype(jnp.bfloat16)
 
     def share(k):
         return lax.dynamic_slice_in_dim(shares, lax.rem(y + k, 4) * cols, cols, 1)

time: 147 us -> 135 us (0.918)
  starting transfers between devices: 54.5 us -> 49.8 us
  waiting for transfers between devices: 28 us -> 25 us
  other arithmetic: 7.5 us -> 4.76 us
  local copies, waits for them, and re-layouts: 7.18 us -> 5.53 us
    ppermute x21, waiting for transfers between devices: 24 us -> 15.1 us  [z_hop(): return lax.ppermute(x, 'group', ring(2 * SPLIT, step, 2))]
    ppermute x3, waiting for transfers between devices: 0.01 us -> 6.41 us  [on_device(): lax.ppermute(share(k), 'tensor', ring(8, k, 2)).astype(jnp.float32)]
    ppermute x1, starting transfers between devices: 8.48 us -> 2.1 us  [on_device(): other = lax.ppermute(theirs, 'tensor', swap(8))]
    select_n x6 -> x5, other arithmetic: 4.84 us -> 0.12 us  [the longest x1 0.04 us: on_device(): down = z_hop(jnp.where(is_owner, piece(3 - half_way), down), -1)]
    concatenate x0 -> x2, other arithmetic: none -> 3.54 us  [the longest x1 1.78 us: on_device(): jnp.concatenate([prefix, prefix], 1)]
    ppermute x1, starting transfers between devices: 7.73 us -> 10.5 us  [on_device(): beside = lax.ppermute(summed, 'tensor', swap(8))]
  transfers between devices with their start and end apart: 28 -> 28, of which waited for: 12 -> 14; matrix products, arithmetic and copies ran while one was open for 6% -> 4% of each run, Pallas kernels for 31% -> 30%
where the time goes in v2:
time: 135 us
  starting transfers between devices  49.8 us (37%)
  Pallas kernels  45.6 us (34%)
  waiting for transfers between devices  25 us (19%)
  local copies, waits for them, and re-layouts  5.53 us (4%)
  other arithmetic  4.76 us (4%)
  between operations  2.98 us (2%)
    pallas_call x6, Pallas kernels, backward(): pl.pallas_call(functools.partial(backward_kernel, kinds, scale, scale2, f...  30.1 us
    ppermute x21, starting transfers between devices, z_hop(): return lax.ppermute(x, 'group', ring(2 * SPLIT, step, 2))  26.6 us
    pallas_call x6, Pallas kernels, forward(): pl.pallas_call(functools.partial(forward_kernel, kinds, scale2, first, la...  15.5 us
    ppermute x21, waiting for transfers between devices, z_hop(): return lax.ppermute(x, 'group', ring(2 * SPLIT, step, 2))  15.1 us
    ppermute x1, starting transfers between devices, on_device(): beside = lax.ppermute(summed, 'tensor', swap(8))  10.5 us
    ppermute x3, waiting for transfers between devices, on_device(): lax.ppermute(share(k), 'tensor', ring(8, k, 2)).astype(jnp.float32)  6.41 us
    ppermute x2, starting transfers between devices, x_swap(): return lax.ppermute(x, 'group', swap(2 * SPLIT))  5.53 us
    ppermute x3, starting transfers between devices, on_device(): lax.ppermute(share(k), 'tensor', ring(8, k, 2)).astype(jnp.float32)  5.07 us
  transfers between devices with their start and end apart: 28, of which 14 were waited for; matrix products, arithmetic and copies ran while one was open for 4% of the time, Pallas kernels for 30%

profile of v2, /device:TPU:1, one launch (start us, length us, event | category | flops | bytes accessed | tf_op | source)
XLA Modules:
  0.0 134.7 jit_solution(7858691434514632588)
XLA Ops:
  0.6 1.8 %fusion = bf16[2,2048,128]{2,1,0:T(8,128)(2,1)S(1)} fusion(s32[]{:T(128)S(6)} %select_n.106, bf16[2,2048,128]{2,1,0:T(8,128)(2,1)} %bitcast.63), kind=kLoop, calls=%fused_computation.6 | loop fusion | flops 2097152 | bytes 2097156 | tf_op jit(solution)/shard_map/concatenate | solution.py:198
  2.5 6.5 %collective-permute-start.1 = (bf16[2,256,128]{2,1,0:T(8,128)(2,1)S(1)}, bf16[2,256,128]{2,1,0:T(8,128)(2,1)S(1)}, u32[]{:S(2)}, u32[]{:S(2)}) collective-permute-start(bf16[2,256,128]{2,1,0:T(8,128)(2,1)S(1)} %slice.64), channel_id=1, source_target_pairs={{0,112},{8,120},{16,0},{24,8},{32,16},{40,24},{48,32},{56,40},{64,... | collective-permute-start | bytes 393224 | tf_op jit(solution)/shard_map/ppermute | solution.py:168
  9.0 0.9 dynamic-slice_bitcast_fusion.2
  10.0 3.1 %dynamic-slice_bitcast_fusion = (bf16[2,4,640,128]{3,2,1,0:T(8,128)(2,1)S(1)}, bf16[2,4,640,128]{3,2,1,0:T(8,128)(2,1)}) fusion(bf16[2,4,2,640,128]{4,3,2,1,0:T(8,128)(2,1)} %bitcast.62, s32[]{:T(128)S(6)} %select_n.111, s32[]{:T(128)S(6)} %select_n.110), kind=kLoop, calls=%fused_computation.4 | loop fusion | bytes 5242888 | tf_op jit(solution)/shard_map/jit(dynamic_index_in_dim)/squeeze | solution.py:206
  13.0 1.9 %collective-permute-done = bf16[2,256,128]{2,1,0:T(8,128)(2,1)S(1)} collective-permute-done((bf16[2,256,128]{2,1,0:T(8,128)(2,1)S(1)}, bf16[2,256,128]{2,1,0:T(8,128)(2,1)S(1)}, u32[]{:S(2)}, u32[]{:S(2)}) %collective-permute-start) | collective-permute-done | bytes 131104 | tf_op jit(solution)/shard_map/ppermute | solution.py:168
  15.0 2.1 %collective-permute-start.4 = (bf16[2,4,640,128]{3,2,1,0:T(8,128)(2,1)}, bf16[2,4,640,128]{3,2,1,0:T(8,128)(2,1)}, u32[]{:S(2)}, u32[]{:S(2)}) collective-permute-start(bf16[2,4,640,128]{3,2,1,0:T(8,128)(2,1)} %get-tuple-element.63), channel_id=1, source_target_pairs={{0,1},{1,0},{2,3},{3,2},{4,5},{5,4},{6,7},{7,6},{8,9},{9,8},{10,11... | collective-permute-start | bytes 3932168 | tf_op jit(solution)/shard_map/ppermute | solution.py:213
  19.2 2.7 %collective-permute-start.3 = (bf16[2,256,128]{2,1,0:T(8,128)(2,1)S(1)}, bf16[2,256,128]{2,1,0:T(8,128)(2,1)S(1)}, u32[]{:S(2)}, u32[]{:S(2)}) collective-permute-start(bf16[2,256,128]{2,1,0:T(8,128)(2,1)S(1)} %get-tuple-element.125), channel_id=1, source_target_pairs={{0,112},{8,120},{16,0},{24,8},{32,16},{40,24},{48,32},{56,40},{64,... | collective-permute-start | bytes 393224 | tf_op jit(solution)/shard_map/ppermute | solution.py:168
  22.0 3.6 %collective-permute-done.2 = bf16[2,256,128]{2,1,0:T(8,128)(2,1)S(1)} collective-permute-done((bf16[2,256,128]{2,1,0:T(8,128)(2,1)S(1)}, bf16[2,256,128]{2,1,0:T(8,128)(2,1)S(1)}, u32[]{:S(2)}, u32[]{:S(2)}) %collective-permute-start.2) | collective-permute-done | bytes 131104 | tf_op jit(solution)/shard_map/ppermute | solution.py:168
  25.5 1.4 %fusion.10 = (bf16[1,4,640,128]{3,2,1,0:T(8,128)(2,1)S(1)}, bf16[1,4,640,128]{3,2,1,0:T(8,128)(2,1)S(1)}) fusion(bf16[2,4,640,128]{3,2,1,0:T(8,128)(2,1)} %collective-permute-done.4), kind=kLoop, calls=%fused_computation.40 | loop fusion | bytes 2621440 | tf_op jit(solution)/shard_map/slice | solution.py:217
  27.1 2.7 %collective-permute-start.7 = (bf16[2,256,128]{2,1,0:T(8,128)(2,1)S(1)}, bf16[2,256,128]{2,1,0:T(8,128)(2,1)S(1)}, u32[]{:S(2)}, u32[]{:S(2)}) collective-permute-start(bf16[2,256,128]{2,1,0:T(8,128)(2,1)S(1)} %get-tuple-element.123), channel_id=1, source_target_pairs={{0,112},{8,120},{16,0},{24,8},{32,16},{40,24},{48,32},{56,40},{64,... | collective-permute-start | bytes 393224 | tf_op jit(solution)/shard_map/ppermute | solution.py:168
  29.7 1.8 %pad_maximum_fusion = bf16[2560,512]{1,0:T(8,128)(2,1)} fusion(bf16[2560,128]{1,0:T(8,128)(2,1)S(1)} %bitcast.61, bf16[2560,128]{1,0:T(8,128)(2,1)S(1)} %bitcast.60, bf16[2560,128]{1,0:T(8,128)(2,1)S(1)} %bitcast.59, bf16[2560,128]{1,0:T(8,128)(2,1)S(1)} %bitcast.58), kind=kLoop, calls=%fused_computation.1 | loop fusion | flops 10485760 | bytes 5242880 | tf_op jit(solution)/shard_map/concatenate | solution.py:217
  31.5 1.0 collective-permute-done.5
  32.7 2.6 %shard_map.103.refs_1_ = f32[4,8,512]{2,1,0:T(8,128)S(1)} custom-call(s32[4]{0:T(128)S(1)} %pad_add_fusion.scal_ref, bf16[512,512]{1,0:T(8,128)(2,1)S(1)} %bitcast.32, bf16[512,512]{1,0:T(8,128)(2,1)S(1)} %bitcast.44, bf16[2,512,128]{2,1,0:T(8,128)(2,1)S(1)} %bitcast.56), custom_call_target="tpu_custom_call" | custom-call | flops 536870912 | bytes 1048576 | tf_op jit(solution)/shard_map/pallas_call | solution.py:75
  35.3 2.3 %collective-permute-done.6 = bf16[2,256,128]{2,1,0:T(8,128)(2,1)S(1)} collective-permute-done((bf16[2,256,128]{2,1,0:T(8,128)(2,1)S(1)}, bf16[2,256,128]{2,1,0:T(8,128)(2,1)S(1)}, u32[]{:S(2)}, u32[]{:S(2)}) %collective-permute-start.6) | collective-permute-done | bytes 131104 | tf_op jit(solution)/shard_map/ppermute | solution.py:168
  37.6 2.8 %collective-permute-start.8 = (bf16[2,256,128]{2,1,0:T(8,128)(2,1)S(1)}, bf16[2,256,128]{2,1,0:T(8,128)(2,1)S(1)}, u32[]{:S(2)}, u32[]{:S(2)}) collective-permute-start(bf16[2,256,128]{2,1,0:T(8,128)(2,1)S(1)} %slice_select_fusion.5), channel_id=1, source_target_pairs={{0,8},{8,0},{16,24},{24,16},{32,40},{40,32},{48,56},{56,48},{64,72... | collective-permute-start | bytes 393224 | tf_op jit(solution)/shard_map/ppermute | solution.py:172
  40.5 2.6 %collective-permute-done.8 = bf16[2,256,128]{2,1,0:T(8,128)(2,1)S(1)} collective-permute-done((bf16[2,256,128]{2,1,0:T(8,128)(2,1)S(1)}, bf16[2,256,128]{2,1,0:T(8,128)(2,1)S(1)}, u32[]{:S(2)}, u32[]{:S(2)}) %collective-permute-start.8) | collective-permute-done | bytes 131104 | tf_op jit(solution)/shard_map/ppermute | solution.py:172
  43.5 1.1 collective-permute-start.9
  44.6 2.2 %shard_map.104.refs_2_ = f32[4,8,512]{2,1,0:T(8,128)S(1)} custom-call(s32[4]{0:T(128)S(1)} %pad_add_fusion.scal_ref, bf16[512,512]{1,0:T(8,128)(2,1)S(1)} %bitcast.33, bf16[512,512]{1,0:T(8,128)(2,1)S(1)} %bitcast.45, bf16[2,256,128]{2,1,0:T(8,128)(2,1)S(1)} %broadcast_select_fusion.refs_0_, f32[4,8,512]{2,1,0:T(8,128)S(1)} %shard_map.103.refs_1_), custom_call_target="tpu_custom_call" | custom-call | flops 268435456 | bytes 1048576 | tf_op jit(solution)/shard_map/pallas_call | solution.py:75
  47.0 1.6 %collective-permute-done.9.refs_0_.refs_1_ = bf16[2,256,128]{2,1,0:T(8,128)(2,1)S(1)} collective-permute-done((bf16[2,256,128]{2,1,0:T(8,128)(2,1)S(1)}, bf16[2,256,128]{2,1,0:T(8,128)(2,1)S(1)}, u32[]{:S(2)}, u32[]{:S(2)}) %collective-permute-start.9) | collective-permute-done | bytes 131104 | tf_op jit(solution)/shard_map/ppermute | solution.py:168
  48.5 2.7 %collective-permute-start.12 = (bf16[2,256,128]{2,1,0:T(8,128)(2,1)S(1)}, bf16[2,256,128]{2,1,0:T(8,128)(2,1)S(1)}, u32[]{:S(2)}, u32[]{:S(2)}) collective-permute-start(bf16[2,256,128]{2,1,0:T(8,128)(2,1)S(1)} %collective-permute-done.10.refs_1_.refs_0_), channel_id=1, source_target_pairs={{0,112},{8,120},{16,0},{24,8},{32,16},{40,24},{48,32},{56,40},{64,... | collective-permute-start | bytes 393224 | tf_op jit(solution)/shard_map/ppermute | solution.py:168
  51.2 2.9 %shard_map.105.refs_2_ = f32[4,8,512]{2,1,0:T(8,128)S(1)} custom-call(s32[4]{0:T(128)S(1)} %pad_add_fusion.scal_ref, bf16[512,512]{1,0:T(8,128)(2,1)S(1)} %bitcast.34, bf16[512,512]{1,0:T(8,128)(2,1)S(1)} %bitcast.46, bf16[2,256,128]{2,1,0:T(8,128)(2,1)S(1)} %collective-permute-done.9.refs_0_.refs_1_, ...), custom_call_target="tpu_custom_call" | custom-call | flops 536870912 | bytes 1048576 | tf_op jit(solution)/shard_map/pallas_call | solution.py:75
  54.4 2.7 %collective-permute-start.14 = (bf16[2,256,128]{2,1,0:T(8,128)(2,1)S(1)}, bf16[2,256,128]{2,1,0:T(8,128)(2,1)S(1)}, u32[]{:S(2)}, u32[]{:S(2)}) collective-permute-start(bf16[2,256,128]{2,1,0:T(8,128)(2,1)S(1)} %collective-permute-done.12.refs_1_.refs_0_), channel_id=1, source_target_pairs={{0,112},{8,120},{16,0},{24,8},{32,16},{40,24},{48,32},{56,40},{64,... | collective-permute-start | bytes 393224 | tf_op jit(solution)/shard_map/ppermute | solution.py:168
  57.1 2.9 %shard_map.106.refs_2_ = f32[4,8,512]{2,1,0:T(8,128)S(1)} custom-call(s32[4]{0:T(128)S(1)} %pad_add_fusion.scal_ref, bf16[512,512]{1,0:T(8,128)(2,1)S(1)} %bitcast.35, bf16[512,512]{1,0:T(8,128)(2,1)S(1)} %bitcast.47, bf16[2,256,128]{2,1,0:T(8,128)(2,1)S(1)} %collective-permute-done.11.refs_0_.refs_1_, ...), custom_call_target="tpu_custom_call" | custom-call | flops 536870912 | bytes 1048576 | tf_op jit(solution)/shard_map/pallas_call | solution.py:75
  59.9 0.6 collective-permute-done.13.refs_0_.refs_1_
  60.5 2.9 %shard_map.107.refs_1_ = f32[4,8,512]{2,1,0:T(8,128)S(1)} custom-call(s32[4]{0:T(128)S(1)} %pad_add_fusion.scal_ref, bf16[512,512]{1,0:T(8,128)(2,1)S(1)} %bitcast.36, bf16[512,512]{1,0:T(8,128)(2,1)S(1)} %bitcast.48, bf16[2,256,128]{2,1,0:T(8,128)(2,1)S(1)} %collective-permute-done.13.refs_0_.refs_1_, ...), custom_call_target="tpu_custom_call" | custom-call | flops 536870912 | bytes 1048576 | tf_op jit(solution)/shard_map/pallas_call | solution.py:75
  63.4 2.2 %collective-permute-done.15.refs_0_ = bf16[2,256,128]{2,1,0:T(8,128)(2,1)S(1)} collective-permute-done((bf16[2,256,128]{2,1,0:T(8,128)(2,1)S(1)}, bf16[2,256,128]{2,1,0:T(8,128)(2,1)S(1)}, u32[]{:S(2)}, u32[]{:S(2)}) %collective-permute-start.15) | collective-permute-done | bytes 131104 | tf_op jit(solution)/shard_map/ppermute | solution.py:168
  65.6 2.2 %shard_map.108.stat_ref = f32[4,8,512]{2,1,0:T(8,128)S(1)} custom-call(s32[4]{0:T(128)S(1)} %pad_add_fusion.scal_ref, bf16[512,512]{1,0:T(8,128)(2,1)S(1)} %bitcast.37, bf16[512,512]{1,0:T(8,128)(2,1)S(1)} %bitcast.49, bf16[2,256,128]{2,1,0:T(8,128)(2,1)S(1)} %collective-permute-done.15.refs_0_, f32[4,8,512]{2,1,0:T(8,128)S(1)} %shard_map.107.refs_1_), custom_call_target="tpu_custom_call" | custom-call | flops 268435456 | bytes 1048576 | tf_op jit(solution)/shard_map/pallas_call | solution.py:75
  67.8 3.5 %shard_map.109 = (f32[512,512]{1,0:T(8,128)S(1)}, bf16[2,256,128]{2,1,0:T(8,128)(2,1)S(1)}) custom-call(s32[4]{0:T(128)S(1)} %pad_add_fusion.scal_ref, bf16[512,512]{1,0:T(8,128)(2,1)S(1)} %bitcast.38, bf16[512,512]{1,0:T(8,128)(2,1)S(1)} %bitcast.50, f32[4,8,512]{2,1,0:T(8,128)S(1)} %shard_map.108.stat_ref, ...), custom_call_target="tpu_custom_call" | custom-call | flops 671088640 | bytes 1048576 | tf_op jit(solution)/shard_map/pallas_call | solution.py:145
  71.4 5.7 %shard_map.110 = (f32[512,512]{1,0:T(8,128)S(1)}, bf16[2,256,128]{2,1,0:T(8,128)(2,1)S(1)}, bf16[2,256,128]{2,1,0:T(8,128)(2,1)S(1)}) custom-call(s32[4]{0:T(128)S(1)} %pad_add_fusion.scal_ref, bf16[512,512]{1,0:T(8,128)(2,1)S(1)} %bitcast.39, bf16[512,512]{1,0:T(8,128)(2,1)S(1)} %bitcast.51, f32[4,8,512]{2,1,0:T(8,128)S(1)} %shard_map.108.stat_ref, ...), custom_call_target="tpu_custom_call" | custom-call | flops 1342177280 | bytes 1048576 | tf_op jit(solution)/shard_map/pallas_call | solution.py:145
  77.5 2.5 %collective-permute-start.20 = (bf16[2,256,128]{2,1,0:T(8,128)(2,1)S(1)}, bf16[2,256,128]{2,1,0:T(8,128)(2,1)S(1)}, u32[]{:S(2)}, u32[]{:S(2)}) collective-permute-start(bf16[2,256,128]{2,1,0:T(8,128)(2,1)S(1)} %get-tuple-element.103), channel_id=1, source_target_pairs={{0,112},{8,120},{16,0},{24,8},{32,16},{40,24},{48,32},{56,40},{64,... | collective-permute-start | bytes 393224 | tf_op jit(solution)/shard_map/ppermute | solution.py:168
  79.9 5.7 %shard_map.111 = (f32[512,512]{1,0:T(8,128)S(1)}, bf16[2,256,128]{2,1,0:T(8,128)(2,1)S(1)}, bf16[2,256,128]{2,1,0:T(8,128)(2,1)S(1)}) custom-call(s32[4]{0:T(128)S(1)} %pad_add_fusion.scal_ref, bf16[512,512]{1,0:T(8,128)(2,1)S(1)} %bitcast.40, bf16[512,512]{1,0:T(8,128)(2,1)S(1)} %bitcast.52, f32[4,8,512]{2,1,0:T(8,128)S(1)} %shard_map.108.stat_ref, ...), custom_call_target="tpu_custom_call" | custom-call | flops 1342177280 | bytes 1048576 | tf_op jit(solution)/shard_map/pallas_call | solution.py:145
  85.8 2.7 %collective-permute-start.21 = (bf16[2,256,128]{2,1,0:T(8,128)(2,1)S(1)}, bf16[2,256,128]{2,1,0:T(8,128)(2,1)S(1)}, u32[]{:S(2)}, u32[]{:S(2)}) collective-permute-start(bf16[2,256,128]{2,1,0:T(8,128)(2,1)S(1)} %add_convert_fusion.2), channel_id=1, source_target_pairs={{0,112},{8,120},{16,0},{24,8},{32,16},{40,24},{48,32},{56,40},{64,... | collective-permute-start | bytes 393224 | tf_op jit(solution)/shard_map/ppermute | solution.py:168
  88.6 5.7 %shard_map.112 = (f32[512,512]{1,0:T(8,128)S(1)}, bf16[2,256,128]{2,1,0:T(8,128)(2,1)S(1)}, bf16[2,256,128]{2,1,0:T(8,128)(2,1)S(1)}) custom-call(s32[4]{0:T(128)S(1)} %pad_add_fusion.scal_ref, bf16[512,512]{1,0:T(8,128)(2,1)S(1)} %bitcast.41, bf16[512,512]{1,0:T(8,128)(2,1)S(1)} %bitcast.53, f32[4,8,512]{2,1,0:T(8,128)S(1)} %shard_map.108.stat_ref, ...), custom_call_target="tpu_custom_call" | custom-call | flops 1342177280 | bytes 1048576 | tf_op jit(solution)/shard_map/pallas_call | solution.py:145
  94.3 0.5 collective-permute-start.22
  94.8 1.3 collective-permute-start.19
  96.2 3.6 %shard_map.113 = (f32[512,512]{1,0:T(8,128)S(1)}, bf16[2,256,128]{2,1,0:T(8,128)(2,1)S(1)}) custom-call(s32[4]{0:T(128)S(1)} %pad_add_fusion.scal_ref, bf16[512,512]{1,0:T(8,128)(2,1)S(1)} %bitcast.42, bf16[512,512]{1,0:T(8,128)(2,1)S(1)} %bitcast.54, f32[4,8,512]{2,1,0:T(8,128)S(1)} %shard_map.108.stat_ref, ...), custom_call_target="tpu_custom_call" | custom-call | flops 671088640 | bytes 1048576 | tf_op jit(solution)/shard_map/pallas_call | solution.py:145
  99.8 1.4 %collective-permute-done.19 = bf16[2,256,128]{2,1,0:T(8,128)(2,1)S(1)} collective-permute-done((bf16[2,256,128]{2,1,0:T(8,128)(2,1)S(1)}, bf16[2,256,128]{2,1,0:T(8,128)(2,1)S(1)}, u32[]{:S(2)}, u32[]{:S(2)}) %collective-permute-start.19) | collective-permute-done | bytes 131104 | tf_op jit(solution)/shard_map/ppermute | solution.py:168
  101.2 2.7 %collective-permute-start.23 = (bf16[2,128,128]{2,1,0:T(8,128)(2,1)S(1)}, bf16[2,128,128]{2,1,0:T(8,128)(2,1)S(1)}, u32[]{:S(2)}, u32[]{:S(2)}) collective-permute-start(bf16[2,128,128]{2,1,0:T(8,128)(2,1)S(1)} %add_convert_fusion.7), channel_id=1, source_target_pairs={{0,8},{8,0},{16,24},{24,16},{32,40},{40,32},{48,56},{56,48},{64,72... | collective-permute-start | bytes 196616 | tf_op jit(solution)/shard_map/ppermute | solution.py:172
  103.9 6.0 %shard_map.114 = (bf16[512,512]{1,0:T(8,128)(2,1)}, bf16[2,512,128]{2,1,0:T(8,128)(2,1)}) custom-call(s32[4]{0:T(128)S(1)} %pad_add_fusion.scal_ref, bf16[512,512]{1,0:T(8,128)(2,1)S(1)} %bitcast.43, bf16[512,512]{1,0:T(8,128)(2,1)S(1)} %bitcast.55, f32[4,8,512]{2,1,0:T(8,128)S(1)} %shard_map.108.stat_ref, bf16[2,512,128]{2,1,0:T(8,128)(2,1)S(1)} %bitcast.57, ...), custom_call_target="tpu_custom_call" | custom-call | flops 1342177280 | bytes 1048576 | tf_op jit(solution)/shard_map/pallas_call | solution.py:145
  110.0 10.5 %collective-permute-start.24 = (bf16[2,128,128]{2,1,0:T(8,128)(2,1)S(1)}, bf16[2,128,128]{2,1,0:T(8,128)(2,1)S(1)}, u32[]{:S(2)}, u32[]{:S(2)}) collective-permute-start(bf16[2,128,128]{2,1,0:T(8,128)(2,1)S(1)} %add_convert_fusion.6), channel_id=1, source_target_pairs={{0,1},{1,0},{2,3},{3,2},{4,5},{5,4},{6,7},{7,6},{8,9},{9,8},{10,11... | collective-permute-start | bytes 196616 | tf_op jit(solution)/shard_map/ppermute | solution.py:267
  120.5 0.9 collective-permute-done.24
  121.4 1.0 convolution_convert_fusion
  122.5 1.4 %collective-permute-start.25 = (bf16[128,640]{1,0:T(8,128)(2,1)S(1)}, bf16[128,640]{1,0:T(8,128)(2,1)S(1)}, u32[]{:S(2)}, u32[]{:S(2)}) collective-permute-start(bf16[128,640]{1,0:T(8,128)(2,1)S(1)} %get-tuple-element.127), channel_id=1, source_target_pairs={{0,2},{1,3},{2,4},{3,5},{4,6},{5,7},{6,0},{7,1},{8,10},{9,11},{10,... | collective-permute-start | bytes 491528 | tf_op jit(solution)/shard_map/ppermute | solution.py:276
  123.9 2.6 %collective-permute-start.26 = (bf16[128,640]{1,0:T(8,128)(2,1)S(1)}, bf16[128,640]{1,0:T(8,128)(2,1)S(1)}, u32[]{:S(2)}, u32[]{:S(2)}) collective-permute-start(bf16[128,640]{1,0:T(8,128)(2,1)S(1)} %get-tuple-element.129), channel_id=1, source_target_pairs={{0,4},{1,5},{2,6},{3,7},{4,0},{5,1},{6,2},{7,3},{8,12},{9,13},{10,... | collective-permute-start | bytes 491528 | tf_op jit(solution)/shard_map/ppermute | solution.py:276
  126.5 1.1 collective-permute-start.27
  127.6 1.8 %collective-permute-done.25 = bf16[128,640]{1,0:T(8,128)(2,1)S(1)} collective-permute-done((bf16[128,640]{1,0:T(8,128)(2,1)S(1)}, bf16[128,640]{1,0:T(8,128)(2,1)S(1)}, u32[]{:S(2)}, u32[]{:S(2)}) %collective-permute-start.25) | collective-permute-done | bytes 163872 | tf_op jit(solution)/shard_map/ppermute | solution.py:276
  129.4 4.6 %collective-permute-done.26 = bf16[128,640]{1,0:T(8,128)(2,1)S(1)} collective-permute-done((bf16[128,640]{1,0:T(8,128)(2,1)S(1)}, bf16[128,640]{1,0:T(8,128)(2,1)S(1)}, u32[]{:S(2)}, u32[]{:S(2)}) %collective-permute-start.26) | collective-permute-done | bytes 163872 | tf_op jit(solution)/shard_map/ppermute | solution.py:276
  134.0 0.8 add_convert_fusion
  (53 shorter events, 2.5 us)
Async XLA Ops:
  2.5 10.6 %collective-permute-start.1 = (bf16[2,256,128]{2,1,0:T(8,128)(2,1)S(1)}, bf16[2,256,128]{2,1,0:T(8,128)(2,1)S(1)}, u32[]{:S(2)}, u32[]{:S(2)}) collective-permute-start(bf16[2,256,128]{2,1,0:T(8,128)(2,1)S(1)} %slice.64), channel_id=1, source_target_pairs={{0,112},{8,120},{16,0},{24,8},{32,16},{40,24},{48,32},{56,40},{64,... | collective-permute-start | bytes 393224 | tf_op jit(solution)/shard_map/ppermute | solution.py:168
  9.9 5.1 %collective-permute-start = (bf16[2,256,128]{2,1,0:T(8,128)(2,1)S(1)}, bf16[2,256,128]{2,1,0:T(8,128)(2,1)S(1)}, u32[]{:S(2)}, u32[]{:S(2)}) collective-permute-start(bf16[2,256,128]{2,1,0:T(8,128)(2,1)S(1)} %dynamic-slice_bitcast_fusion.2), channel_id=1, source_target_pairs={{0,16},{8,24},{16,32},{24,40},{32,48},{40,56},{48,64},{56,72},{64,... | collective-permute-start | bytes 393224 | tf_op jit(solution)/shard_map/ppermute | solution.py:168
  15.0 10.6 %collective-permute-start.4 = (bf16[2,4,640,128]{3,2,1,0:T(8,128)(2,1)}, bf16[2,4,640,128]{3,2,1,0:T(8,128)(2,1)}, u32[]{:S(2)}, u32[]{:S(2)}) collective-permute-start(bf16[2,4,640,128]{3,2,1,0:T(8,128)(2,1)} %get-tuple-element.63), channel_id=1, source_target_pairs={{0,1},{1,0},{2,3},{3,2},{4,5},{5,4},{6,7},{7,6},{8,9},{9,8},{10,11... | collective-permute-start | bytes 3932168 | tf_op jit(solution)/shard_map/ppermute | solution.py:213
  19.1 6.4 %collective-permute-start.2 = (bf16[2,256,128]{2,1,0:T(8,128)(2,1)S(1)}, bf16[2,256,128]{2,1,0:T(8,128)(2,1)S(1)}, u32[]{:S(2)}, u32[]{:S(2)}) collective-permute-start(bf16[2,256,128]{2,1,0:T(8,128)(2,1)S(1)} %get-tuple-element.126), channel_id=1, source_target_pairs={{0,16},{8,24},{16,32},{24,40},{32,48},{40,56},{48,64},{56,72},{64,... | collective-permute-start | bytes 393224 | tf_op jit(solution)/shard_map/ppermute | solution.py:168
  19.2 6.3 %collective-permute-start.3 = (bf16[2,256,128]{2,1,0:T(8,128)(2,1)S(1)}, bf16[2,256,128]{2,1,0:T(8,128)(2,1)S(1)}, u32[]{:S(2)}, u32[]{:S(2)}) collective-permute-start(bf16[2,256,128]{2,1,0:T(8,128)(2,1)S(1)} %get-tuple-element.125), channel_id=1, source_target_pairs={{0,112},{8,120},{16,0},{24,8},{32,16},{40,24},{48,32},{56,40},{64,... | collective-permute-start | bytes 393224 | tf_op jit(solution)/shard_map/ppermute | solution.py:168
  27.0 5.5 %collective-permute-start.5 = (bf16[2,256,128]{2,1,0:T(8,128)(2,1)S(1)}, bf16[2,256,128]{2,1,0:T(8,128)(2,1)S(1)}, u32[]{:S(2)}, u32[]{:S(2)}) collective-permute-start(bf16[2,256,128]{2,1,0:T(8,128)(2,1)S(1)} %get-tuple-element.124), channel_id=1, source_target_pairs={{0,16},{8,24},{16,32},{24,40},{32,48},{40,56},{48,64},{56,72},{64,... | collective-permute-start | bytes 393224 | tf_op jit(solution)/shard_map/ppermute | solution.py:168
  27.1 10.6 %collective-permute-start.7 = (bf16[2,256,128]{2,1,0:T(8,128)(2,1)S(1)}, bf16[2,256,128]{2,1,0:T(8,128)(2,1)S(1)}, u32[]{:S(2)}, u32[]{:S(2)}) collective-permute-start(bf16[2,256,128]{2,1,0:T(8,128)(2,1)S(1)} %get-tuple-element.123), channel_id=1, source_target_pairs={{0,112},{8,120},{16,0},{24,8},{32,16},{40,24},{48,32},{56,40},{64,... | collective-permute-start | bytes 393224 | tf_op jit(solution)/shard_map/ppermute | solution.py:168
  29.7 3.0 %copy-start = (bf16[1,512,512]{2,1,0:T(8,128)(2,1)S(1)}, bf16[1,512,512]{2,1,0:T(8,128)(2,1)}, u32[]{:S(2)}) copy-start(bf16[1,512,512]{2,1,0:T(8,128)(2,1)} %param.8) | copy-start | bytes 1572868
  29.7 3.0 %copy-start.1 = (bf16[1,512,512]{2,1,0:T(8,128)(2,1)S(1)}, bf16[1,512,512]{2,1,0:T(8,128)(2,1)}, u32[]{:S(2)}) copy-start(bf16[1,512,512]{2,1,0:T(8,128)(2,1)} %param.10) | copy-start | bytes 1572868
  29.7 3.0 %copy-start.2 = (bf16[1,2,512,128]{3,2,1,0:T(8,128)(2,1)S(1)}, bf16[1,2,512,128]{3,2,1,0:T(8,128)(2,1)}, u32[]{:S(2)}) copy-start(bf16[1,2,512,128]{3,2,1,0:T(8,128)(2,1)} %param.9) | copy-start | bytes 786436
  32.5 5.1 %collective-permute-start.6 = (bf16[2,256,128]{2,1,0:T(8,128)(2,1)S(1)}, bf16[2,256,128]{2,1,0:T(8,128)(2,1)S(1)}, u32[]{:S(2)}, u32[]{:S(2)}) collective-permute-start(bf16[2,256,128]{2,1,0:T(8,128)(2,1)S(1)} %slice_select_fusion.4), channel_id=1, source_target_pairs={{0,16},{8,24},{16,32},{24,40},{32,48},{40,56},{48,64},{56,72},{64,... | collective-permute-start | bytes 393224 | tf_op jit(solution)/shard_map/ppermute | solution.py:168
  37.6 5.4 %collective-permute-start.8 = (bf16[2,256,128]{2,1,0:T(8,128)(2,1)S(1)}, bf16[2,256,128]{2,1,0:T(8,128)(2,1)S(1)}, u32[]{:S(2)}, u32[]{:S(2)}) collective-permute-start(bf16[2,256,128]{2,1,0:T(8,128)(2,1)S(1)} %slice_select_fusion.5), channel_id=1, source_target_pairs={{0,8},{8,0},{16,24},{24,16},{32,40},{40,32},{48,56},{56,48},{64,72... | collective-permute-start | bytes 393224 | tf_op jit(solution)/shard_map/ppermute | solution.py:172
  43.1 3.9 %collective-permute-start.10 = (bf16[2,256,128]{2,1,0:T(8,128)(2,1)S(1)}, bf16[2,256,128]{2,1,0:T(8,128)(2,1)S(1)}, u32[]{:S(2)}, u32[]{:S(2)}) collective-permute-start(bf16[2,256,128]{2,1,0:T(8,128)(2,1)S(1)} %broadcast_select_fusion.refs_0_), channel_id=1, source_target_pairs={{0,112},{8,120},{16,0},{24,8},{32,16},{40,24},{48,32},{56,40},{64,... | collective-permute-start | bytes 393224 | tf_op jit(solution)/shard_map/ppermute | solution.py:168
  43.5 5.0 %collective-permute-start.9 = (bf16[2,256,128]{2,1,0:T(8,128)(2,1)S(1)}, bf16[2,256,128]{2,1,0:T(8,128)(2,1)S(1)}, u32[]{:S(2)}, u32[]{:S(2)}) collective-permute-start(bf16[2,256,128]{2,1,0:T(8,128)(2,1)S(1)} %broadcast_select_fusion.refs_0_), channel_id=1, source_target_pairs={{0,16},{8,24},{16,32},{24,40},{32,48},{40,56},{48,64},{56,72},{64,... | collective-permute-start | bytes 393224 | tf_op jit(solution)/shard_map/ppermute | solution.py:168
  48.5 5.8 %collective-permute-start.11 = (bf16[2,256,128]{2,1,0:T(8,128)(2,1)S(1)}, bf16[2,256,128]{2,1,0:T(8,128)(2,1)S(1)}, u32[]{:S(2)}, u32[]{:S(2)}) collective-permute-start(bf16[2,256,128]{2,1,0:T(8,128)(2,1)S(1)} %collective-permute-done.9.refs_0_.refs_1_), channel_id=1, source_target_pairs={{0,16},{8,24},{16,32},{24,40},{32,48},{40,56},{48,64},{56,72},{64,... | collective-permute-start | bytes 393224 | tf_op jit(solution)/shard_map/ppermute | solution.py:168
  48.5 5.8 %collective-permute-start.12 = (bf16[2,256,128]{2,1,0:T(8,128)(2,1)S(1)}, bf16[2,256,128]{2,1,0:T(8,128)(2,1)S(1)}, u32[]{:S(2)}, u32[]{:S(2)}) collective-permute-start(bf16[2,256,128]{2,1,0:T(8,128)(2,1)S(1)} %collective-permute-done.10.refs_1_.refs_0_), channel_id=1, source_target_pairs={{0,112},{8,120},{16,0},{24,8},{32,16},{40,24},{48,32},{56,40},{64,... | collective-permute-start | bytes 393224 | tf_op jit(solution)/shard_map/ppermute | solution.py:168
  54.4 6.2 %collective-permute-start.13 = (bf16[2,256,128]{2,1,0:T(8,128)(2,1)S(1)}, bf16[2,256,128]{2,1,0:T(8,128)(2,1)S(1)}, u32[]{:S(2)}, u32[]{:S(2)}) collective-permute-start(bf16[2,256,128]{2,1,0:T(8,128)(2,1)S(1)} %collective-permute-done.11.refs_0_.refs_1_), channel_id=1, source_target_pairs={{0,16},{8,24},{16,32},{24,40},{32,48},{40,56},{48,64},{56,72},{64,... | collective-permute-start | bytes 393224 | tf_op jit(solution)/shard_map/ppermute | solution.py:168
  54.4 6.2 %collective-permute-start.14 = (bf16[2,256,128]{2,1,0:T(8,128)(2,1)S(1)}, bf16[2,256,128]{2,1,0:T(8,128)(2,1)S(1)}, u32[]{:S(2)}, u32[]{:S(2)}) collective-permute-start(bf16[2,256,128]{2,1,0:T(8,128)(2,1)S(1)} %collective-permute-done.12.refs_1_.refs_0_), channel_id=1, source_target_pairs={{0,112},{8,120},{16,0},{24,8},{32,16},{40,24},{48,32},{56,40},{64,... | collective-permute-start | bytes 393224 | tf_op jit(solution)/shard_map/ppermute | solution.py:168
  60.5 5.0 %collective-permute-start.15 = (bf16[2,256,128]{2,1,0:T(8,128)(2,1)S(1)}, bf16[2,256,128]{2,1,0:T(8,128)(2,1)S(1)}, u32[]{:S(2)}, u32[]{:S(2)}) collective-permute-start(bf16[2,256,128]{2,1,0:T(8,128)(2,1)S(1)} %collective-permute-done.13.refs_0_.refs_1_), channel_id=1, source_target_pairs={{0,16},{8,24},{16,32},{24,40},{32,48},{40,56},{48,64},{56,72},{64,... | collective-permute-start | bytes 393224 | tf_op jit(solution)/shard_map/ppermute | solution.py:168
  71.3 5.8 %collective-permute-start.16 = (bf16[2,256,128]{2,1,0:T(8,128)(2,1)S(1)}, bf16[2,256,128]{2,1,0:T(8,128)(2,1)S(1)}, u32[]{:S(2)}, u32[]{:S(2)}) collective-permute-start(bf16[2,256,128]{2,1,0:T(8,128)(2,1)S(1)} %get-tuple-element.82), channel_id=1, source_target_pairs={{0,16},{8,24},{16,32},{24,40},{32,48},{40,56},{48,64},{56,72},{64,... | collective-permute-start | bytes 393224 | tf_op jit(solution)/shard_map/ppermute | solution.py:168
  77.1 8.5 %collective-permute-start.17 = (bf16[2,256,128]{2,1,0:T(8,128)(2,1)S(1)}, bf16[2,256,128]{2,1,0:T(8,128)(2,1)S(1)}, u32[]{:S(2)}, u32[]{:S(2)}) collective-permute-start(bf16[2,256,128]{2,1,0:T(8,128)(2,1)S(1)} %add_convert_fusion.5), channel_id=1, source_target_pairs={{0,16},{8,24},{16,32},{24,40},{32,48},{40,56},{48,64},{56,72},{64,... | collective-permute-start | bytes 393224 | tf_op jit(solution)/shard_map/ppermute | solution.py:168
  77.5 8.3 %collective-permute-start.20 = (bf16[2,256,128]{2,1,0:T(8,128)(2,1)S(1)}, bf16[2,256,128]{2,1,0:T(8,128)(2,1)S(1)}, u32[]{:S(2)}, u32[]{:S(2)}) collective-permute-start(bf16[2,256,128]{2,1,0:T(8,128)(2,1)S(1)} %get-tuple-element.103), channel_id=1, source_target_pairs={{0,112},{8,120},{16,0},{24,8},{32,16},{40,24},{48,32},{56,40},{64,... | collective-permute-start | bytes 393224 | tf_op jit(solution)/shard_map/ppermute | solution.py:168
  85.7 8.6 %collective-permute-start.18 = (bf16[2,256,128]{2,1,0:T(8,128)(2,1)S(1)}, bf16[2,256,128]{2,1,0:T(8,128)(2,1)S(1)}, u32[]{:S(2)}, u32[]{:S(2)}) collective-permute-start(bf16[2,256,128]{2,1,0:T(8,128)(2,1)S(1)} %add_convert_fusion.4), channel_id=1, source_target_pairs={{0,16},{8,24},{16,32},{24,40},{32,48},{40,56},{48,64},{56,72},{64,... | collective-permute-start | bytes 393224 | tf_op jit(solution)/shard_map/ppermute | solution.py:168
  85.8 8.4 %collective-permute-start.21 = (bf16[2,256,128]{2,1,0:T(8,128)(2,1)S(1)}, bf16[2,256,128]{2,1,0:T(8,128)(2,1)S(1)}, u32[]{:S(2)}, u32[]{:S(2)}) collective-permute-start(bf16[2,256,128]{2,1,0:T(8,128)(2,1)S(1)} %add_convert_fusion.2), channel_id=1, source_target_pairs={{0,112},{8,120},{16,0},{24,8},{32,16},{40,24},{48,32},{56,40},{64,... | collective-permute-start | bytes 393224 | tf_op jit(solution)/shard_map/ppermute | solution.py:168
  94.3 5.4 %collective-permute-start.22 = (bf16[2,256,128]{2,1,0:T(8,128)(2,1)S(1)}, bf16[2,256,128]{2,1,0:T(8,128)(2,1)S(1)}, u32[]{:S(2)}, u32[]{:S(2)}) collective-permute-start(bf16[2,256,128]{2,1,0:T(8,128)(2,1)S(1)} %add_convert_fusion.1), channel_id=1, source_target_pairs={{0,112},{8,120},{16,0},{24,8},{32,16},{40,24},{48,32},{56,40},{64,... | collective-permute-start | bytes 393224 | tf_op jit(solution)/shard_map/ppermute | solution.py:168
  94.8 6.3 %collective-permute-start.19 = (bf16[2,256,128]{2,1,0:T(8,128)(2,1)S(1)}, bf16[2,256,128]{2,1,0:T(8,128)(2,1)S(1)}, u32[]{:S(2)}, u32[]{:S(2)}) collective-permute-start(bf16[2,256,128]{2,1,0:T(8,128)(2,1)S(1)} %add_convert_fusion.3), channel_id=1, source_target_pairs={{0,16},{8,24},{16,32},{24,40},{32,48},{40,56},{48,64},{56,72},{64,... | collective-permute-start | bytes 393224 | tf_op jit(solution)/shard_map/ppermute | solution.py:168
  101.2 20.2 %copy-start.3 = (bf16[2560,512]{1,0:T(8,128)(2,1)S(1)}, bf16[2560,512]{1,0:T(8,128)(2,1)}, u32[]{:S(2)}) copy-start(bf16[2560,512]{1,0:T(8,128)(2,1)} %pad_maximum_fusion) | copy-start | bytes 7864324
  101.2 8.7 %collective-permute-start.23 = (bf16[2,128,128]{2,1,0:T(8,128)(2,1)S(1)}, bf16[2,128,128]{2,1,0:T(8,128)(2,1)S(1)}, u32[]{:S(2)}, u32[]{:S(2)}) collective-permute-start(bf16[2,128,128]{2,1,0:T(8,128)(2,1)S(1)} %add_convert_fusion.7), channel_id=1, source_target_pairs={{0,8},{8,0},{16,24},{24,16},{32,40},{40,32},{48,56},{56,48},{64,72... | collective-permute-start | bytes 196616 | tf_op jit(solution)/shard_map/ppermute | solution.py:172
  110.0 11.4 %collective-permute-start.24 = (bf16[2,128,128]{2,1,0:T(8,128)(2,1)S(1)}, bf16[2,128,128]{2,1,0:T(8,128)(2,1)S(1)}, u32[]{:S(2)}, u32[]{:S(2)}) collective-permute-start(bf16[2,128,128]{2,1,0:T(8,128)(2,1)S(1)} %add_convert_fusion.6), channel_id=1, source_target_pairs={{0,1},{1,0},{2,3},{3,2},{4,5},{5,4},{6,7},{7,6},{8,9},{9,8},{10,11... | collective-permute-start | bytes 196616 | tf_op jit(solution)/shard_map/ppermute | solution.py:267
  122.5 6.9 %collective-permute-start.25 = (bf16[128,640]{1,0:T(8,128)(2,1)S(1)}, bf16[128,640]{1,0:T(8,128)(2,1)S(1)}, u32[]{:S(2)}, u32[]{:S(2)}) collective-permute-start(bf16[128,640]{1,0:T(8,128)(2,1)S(1)} %get-tuple-element.127), channel_id=1, source_target_pairs={{0,2},{1,3},{2,4},{3,5},{4,6},{5,7},{6,0},{7,1},{8,10},{9,11},{10,... | collective-permute-start | bytes 491528 | tf_op jit(solution)/shard_map/ppermute | solution.py:276
  123.9 10.1 %collective-permute-start.26 = (bf16[128,640]{1,0:T(8,128)(2,1)S(1)}, bf16[128,640]{1,0:T(8,128)(2,1)S(1)}, u32[]{:S(2)}, u32[]{:S(2)}) collective-permute-start(bf16[128,640]{1,0:T(8,128)(2,1)S(1)} %get-tuple-element.129), channel_id=1, source_target_pairs={{0,4},{1,5},{2,6},{3,7},{4,0},{5,1},{6,2},{7,3},{8,12},{9,13},{10,... | collective-permute-start | bytes 491528 | tf_op jit(solution)/shard_map/ppermute | solution.py:276
  126.5 7.5 %collective-permute-start.27 = (bf16[128,640]{1,0:T(8,128)(2,1)S(1)}, bf16[128,640]{1,0:T(8,128)(2,1)S(1)}, u32[]{:S(2)}, u32[]{:S(2)}) collective-permute-start(bf16[128,640]{1,0:T(8,128)(2,1)S(1)} %get-tuple-element.128), channel_id=1, source_target_pairs={{0,6},{1,7},{2,0},{3,1},{4,2},{5,3},{6,4},{7,5},{8,14},{9,15},{10,... | collective-permute-start | bytes 491528 | tf_op jit(solution)/shard_map/ppermute | solution.py:276
